TPU v7x, 256 devices: a whole 4x4x8 slice. The times are simulated.
256 devices in a mesh: branch: 2 (over core), head: 8 (over z), seq: 16 (over y, x).
Axes of the slice: x: 4, y: 4, z: 8, core: 2. Of those that a mesh axis runs over, the one named last changes fastest.
Arguments:
- hidden: bfloat16 [2, 16384, 3072], P('branch', 'seq', 'head'), may hold values from -4.1875 to 4.1875
- modulation: float32 [2, 3, 3072], P('branch'), may hold values from 0.3 to 1.5
- branch_cache: bfloat16 [2, 16384, 3072], P('branch', 'seq', 'head'), may hold values from -4.78125 to 4.78125
- k_cache: bfloat16 [2, 16384, 2048], P('branch', 'seq', 'head'), may hold values from -136 to 136
- v_cache: bfloat16 [2, 16384, 2048], P('branch', 'seq', 'head'), may hold values from -6 to 6
- w_qkv: bfloat16 [3072, 3, 2048], P('branch', None, 'head'), may hold values from -0.109375 to 0.109375
- w_mlp_in: bfloat16 [3072, 6144], P('branch', 'head'), may hold values from -0.109375 to 0.109375
- w_attn_out: bfloat16 [2048, 3072], P('head', 'branch'), may hold values from -0.125 to 0.125
- w_mlp_out: bfloat16 [6144, 3072], P('head', 'branch'), may hold values from -0.078125 to 0.078125
- q_gain: float32 [128], replicated, may hold values from 1 to 3
- k_gain: float32 [128], replicated, may hold values from 1 to 3
- blocks: int32 [16, 2], P('seq'), may hold values from 0 to 7, as said below
- counts: int32 [16], P('seq'), may hold values from 1 to 2, as said below
Outputs:
- guided: bfloat16 [16384, 3072], P('seq', 'head')
Inputs may be any that keep to these rules, and one draw needn't show every extreme that they name: `blocks`: each row holds 2 different block numbers; only the first counts[r] of row r are live. `counts`: some index of seq has 2 live blocks and some has 1.
All inputs are finite; a program needn't handle non-finite values.
Results may differ from a plain program's by a relative error of at most 0.015.
The roundings to bfloat16 on the way count: a program that leaves them out, or rounds other values in their place, can miss the bound.
Values may be sent and summed in bfloat16 or wider, within the bound.
No kernel may reach another device: no remote copies, remote signals or barrier semaphores. Data moves between devices by JAX's collectives and lax.ppermute only.
A program may use at most 192 MiB of HBM per device.

v0:
```python
import functools

import jax
import jax.numpy as jnp
from jax import lax
from jax.experimental import pallas as pl
from jax.experimental.pallas import tpu as pltpu
from jax.sharding import Mesh, PartitionSpec as P

HDIM = 128
BLOCK = 128
GUIDANCE = 1.5
EPSILON = 1e-06
LOG2E = 1.4426950408889634
HEAD = 8
SIDE = 4
STALE = 6
STAT_ROWS = 16
MIB = 1024 * 1024

F32 = jnp.float32
BF16 = jnp.bfloat16


def whole():
    return pl.BlockSpec(memory_space=pltpu.VMEM)


def scalars():
    return pl.BlockSpec(memory_space=pltpu.SMEM)


def in_hbm():
    return pl.BlockSpec(memory_space=pltpu.HBM)


def anywhere():
    return pl.BlockSpec(memory_space=pl.ANY)


def params(mebibytes=58):
    return pltpu.CompilerParams(vmem_limit_bytes=mebibytes * MIB)


def dot(left, right):
    return jnp.dot(left, right, preferred_element_type=F32)


def begin(pairs, arrived):
    copies = [
        pltpu.make_async_copy(source, target, arrived.at[i])
        for i, (source, target) in enumerate(pairs)
    ]
    for copy in copies:
        copy.start()
    return copies


def block_rows(number):
    return pl.ds(pl.multiple_of(number * BLOCK, BLOCK), BLOCK)


def pick_kernel(blocks_ref, counts_ref, tokens_ref, k_ref, v_ref, *refs):
    out_ref, packed, (stale_s, arrived, sent) = refs[0], refs[1:3], refs[3:]
    pairs = [
        (tokens_ref.at[block_rows(blocks_ref[0, j])], out_ref.at[pl.ds(j * BLOCK, BLOCK)])
        for j in range(2)
    ]
    low = jnp.minimum(blocks_ref[0, 0], blocks_ref[0, 1])
    high = jnp.maximum(blocks_ref[0, 0], blocks_ref[0, 1])
    for i in range(STALE):
        index = i + (i >= low).astype(jnp.int32)
        index = index + (index >= high).astype(jnp.int32)
        for half, ref in enumerate((k_ref, v_ref)):
            pairs.append((ref.at[block_rows(index)], stale_s.at[half, pl.ds(i * BLOCK, BLOCK)]))
    copies = begin(pairs, arrived)
    for copy in copies[2:]:
        copy.wait()
    pairs = [
        (stale_s.at[half, :, pl.ds(head * HDIM, HDIM)], packed[head].at[:, pl.ds(half * HDIM, HDIM)])
        for head in range(2)
        for half in range(2)
    ]
    for copy in copies[:2] + begin(pairs, sent):
        copy.wait()


def pick(tokens, keys, values, blocks, counts):
    shape = jax.ShapeDtypeStruct((2 * BLOCK, tokens.shape[1]), BF16)
    stale = jax.ShapeDtypeStruct((STALE * BLOCK, 2 * HDIM), BF16)
    return pl.pallas_call(
        pick_kernel,
        in_specs=[scalars(), scalars()] + [in_hbm()] * 3,
        out_specs=[whole()] + [in_hbm()] * 2,
        out_shape=[shape, stale, stale],
        scratch_shapes=[
            pltpu.VMEM((2, STALE * BLOCK, 2 * HDIM), BF16),
            pltpu.SemaphoreType.DMA((2 + 2 * STALE,)),
            pltpu.SemaphoreType.DMA((4,)),
        ],
        compiler_params=params(),
        name="pick",
    )(blocks, counts, tokens, keys, values)


def project_kernel(blocks_ref, counts_ref, *refs):
    sources = refs[: HEAD + 5]
    keys_ref, values_ref = refs[HEAD + 5 : HEAD + 7]
    x_ref, y_ref, rows_ref = refs[HEAD + 7 : HEAD + 10]
    chunk_s, mod_ref, own_ref, other_ref, q_gain_ref, k_gain_ref, old_s, arrived = refs[HEAD + 10 :]
    core = lax.axis_index("branch")
    z = lax.axis_index("head")
    old = block_rows(blocks_ref[0, 1])
    targets = [chunk_s.at[k] for k in range(HEAD)]
    targets += [mod_ref, own_ref, other_ref, q_gain_ref, k_gain_ref]
    pairs = list(zip(sources, targets))
    pairs += [(keys_ref.at[old], old_s.at[0]), (values_ref.at[old], old_s.at[1])]
    copies = begin(pairs, arrived)
    for copy in copies[: HEAD + 1]:
        copy.wait()
    width = chunk_s.shape[2]
    full = HEAD * width
    step = 32
    for row in range(0, 2 * BLOCK, step):
        values = [chunk_s[k, row : row + step, :].astype(F32) for k in range(HEAD)]
        mean = sum(jnp.sum(v, axis=-1, keepdims=True) for v in values) / full
        centred = [v - mean for v in values]
        var = sum(jnp.sum(c * c, axis=-1, keepdims=True) for c in centred) / full
        inverse = lax.rsqrt(var + EPSILON)
        for k in range(HEAD):
            owner = lax.rem(z - k + HEAD, HEAD)
            columns = pl.ds(pl.multiple_of(owner * width, width), width)
            shift = mod_ref[0, :, columns]
            scale = mod_ref[1, :, columns]
            rows_ref[row : row + step, columns] = (
                centred[k] * inverse * (1.0 + scale) + shift
            ).astype(BF16)
    for copy in copies[HEAD + 1 :]:
        copy.wait()
    half = full // 2
    here = pl.ds(pl.multiple_of(core * half, half), half)
    there = pl.ds(pl.multiple_of((1 - core) * half, half), half)
    query, key, value = (
        dot(rows_ref[:, here], own_ref[i]) + dot(rows_ref[:, there], other_ref[i]) for i in range(3)
    )

    def norm(values, gain_ref):
        power = jnp.mean(values * values, axis=-1, keepdims=True)
        return (values * lax.rsqrt(power + EPSILON) * gain_ref[...]).astype(BF16)

    live = counts_ref[0] > 1
    for head, fresh_ref, query_ref in ((0, x_ref, y_ref), (1, y_ref, x_ref)):
        at = head * HDIM
        query_ref[:, 2 * HDIM :] = norm(query[:, at : at + HDIM], q_gain_ref)
        new_key = norm(key[:, at : at + HDIM], k_gain_ref)
        new_value = value[:, at : at + HDIM].astype(BF16)
        fresh_ref[:BLOCK, :HDIM] = new_key[:BLOCK]
        fresh_ref[:BLOCK, HDIM : 2 * HDIM] = new_value[:BLOCK]
        fresh_ref[BLOCK:, :HDIM] = jnp.where(live, new_key[BLOCK:], old_s[0, :, at : at + HDIM])
        fresh_ref[BLOCK:, HDIM : 2 * HDIM] = jnp.where(
            live, new_value[BLOCK:], old_s[1, :, at : at + HDIM]
        )


def project(blocks, counts, chunks, mod, own, other, q_gain, k_gain, keys, values):
    rows, width = chunks[0].shape
    full = HEAD * width
    sources = [*chunks, mod, own, other, q_gain, k_gain, keys, values]
    return pl.pallas_call(
        project_kernel,
        in_specs=[scalars()] * 2 + [in_hbm()] * len(sources),
        out_specs=[whole()] * 3,
        out_shape=[
            jax.ShapeDtypeStruct((rows, 3 * HDIM), BF16),
            jax.ShapeDtypeStruct((rows, 3 * HDIM), BF16),
            jax.ShapeDtypeStruct((rows, full), BF16),
        ],
        scratch_shapes=[
            pltpu.VMEM((HEAD, rows, width), BF16),
            *[pltpu.VMEM(a.shape, a.dtype) for a in (mod, own, other, q_gain, k_gain)],
            pltpu.VMEM((2, BLOCK, 2 * HDIM), BF16),
            pltpu.SemaphoreType.DMA((len(sources),)),
        ],
        compiler_params=params(),
        cost_estimate=pl.CostEstimate(
            flops=2 * rows * full * 6 * HDIM, bytes_accessed=8 * MIB, transcendentals=0
        ),
        name="project",
    )(blocks, counts, *sources)


def hidden_kernel(rows_ref, own_ref, other_ref, mine_ref, theirs_ref):
    core = lax.axis_index("branch")
    half = own_ref.shape[0]
    here = pl.ds(pl.multiple_of(core * half, half), half)
    there = pl.ds(pl.multiple_of((1 - core) * half, half), half)
    total = dot(rows_ref[:, here], own_ref[...]) + dot(rows_ref[:, there], other_ref[...])
    active = jax.nn.gelu(total, approximate=True).astype(BF16)
    first = core == 0
    mine_ref[...] = jnp.where(first, active[:BLOCK], active[BLOCK:])
    theirs_ref[...] = jnp.where(first, active[BLOCK:], active[:BLOCK])


def hidden_units(rows, own, other):
    units = own.shape[1]
    shape = jax.ShapeDtypeStruct((BLOCK, units), BF16)
    return pl.pallas_call(
        hidden_kernel,
        in_specs=[whole()] * 3,
        out_specs=[whole()] * 2,
        out_shape=[shape, shape],
        compiler_params=params(14),
        cost_estimate=pl.CostEstimate(
            flops=2 * rows.shape[0] * rows.shape[1] * units,
            bytes_accessed=8 * MIB,
            transcendentals=rows.shape[0] * units,
        ),
        name="hidden_units",
    )(rows, own, other)


def gated(mine_ref, theirs_ref, w_own, w_other, mod_own, mod_other, emit):
    core = lax.axis_index("branch")
    factor = jnp.where(core == 0, 1.0 - GUIDANCE, GUIDANCE)
    width = w_own.shape[1] // (HEAD // 2)
    left = jnp.concatenate([mine_ref[...], theirs_ref[...]], axis=0)
    for weights, side in ((w_own, core), (w_other, 1 - core)):
        both = dot(left, weights[...])
        for i in range(HEAD // 2):
            part = both[:, i * width : (i + 1) * width]
            chunk = side * (HEAD // 2) + i
            columns = pl.ds(pl.multiple_of(chunk * width, width), width)
            gate_own = factor * mod_own[2, :, columns]
            gate_other = (1.0 - factor) * mod_other[2, :, columns]
            emit(chunk, part[:BLOCK] * gate_own + part[BLOCK:] * gate_other)


def units_out_kernel(mine_ref, theirs_ref, own_ref, other_ref, mod_ref, mod_other_ref, out_ref):
    def emit(chunk, value):
        out_ref[chunk] = value

    gated(mine_ref, theirs_ref, own_ref, other_ref, mod_ref, mod_other_ref, emit)


def heads_out_kernel(
    mine_ref, theirs_ref, own_ref, other_ref, mod_ref, mod_other_ref, base_ref, out_ref
):
    def emit(chunk, value):
        out_ref[chunk] = (base_ref[chunk] + value).astype(BF16)

    gated(mine_ref, theirs_ref, own_ref, other_ref, mod_ref, mod_other_ref, emit)


def out_product(kernel, dtype, name, limit, mine, theirs, own, other, mod, mod_other, *base):
    width = own.shape[1] // (HEAD // 2)
    return pl.pallas_call(
        kernel,
        in_specs=[whole()] * (6 + len(base)),
        out_specs=whole(),
        out_shape=jax.ShapeDtypeStruct((HEAD, BLOCK, width), dtype),
        compiler_params=params(limit),
        cost_estimate=pl.CostEstimate(
            flops=8 * BLOCK * own.shape[0] * own.shape[1],
            bytes_accessed=6 * MIB,
            transcendentals=0,
        ),
        name=name,
    )(mine, theirs, own, other, mod, mod_other, *base)


def attend_kernel(*refs):
    stale_ref = refs[0]
    fresh, asked = refs[1 : 1 + SIDE], refs[1 + SIDE : 1 + 2 * SIDE]
    outs = refs[-9:-5]
    key_s, score_s, query_s, stat_s, arrived = refs[-5:]
    rows = 2 * BLOCK
    keys = key_s.shape[0]
    tiles = 4
    piece = keys // tiles
    unit = LOG2E * HDIM**-0.5
    old = stale_ref.shape[0]
    pairs = [(asked[k].at[:, pl.ds(2 * HDIM, HDIM)], query_s.at[k]) for k in range(SIDE)]
    pairs += [
        (fresh[k].at[:, pl.ds(0, 2 * HDIM)], key_s.at[pl.ds(old + k * rows, rows)])
        for k in range(SIDE)
    ]
    pairs.append((stale_ref, key_s.at[pl.ds(0, old)]))
    for copy in begin(pairs, arrived):
        copy.wait()
    stat_s[...] = jnp.zeros_like(stat_s)

    def tile(index, carry):
        query = query_s[index]
        top = None
        for k in range(tiles):
            part = key_s[k * piece : (k + 1) * piece, :HDIM]
            scores = lax.dot_general(
                query, part, (((1,), (1,)), ((), ())), preferred_element_type=F32
            )
            score_s[:, k * piece : (k + 1) * piece] = scores
            here = jnp.max(scores, axis=-1, keepdims=True)
            top = here if top is None else jnp.maximum(top, here)
        top = top * unit
        total = jnp.zeros((rows, 1), F32)
        summed = jnp.zeros((rows, HDIM), F32)
        for k in range(tiles):
            weights = jnp.exp2(score_s[:, k * piece : (k + 1) * piece] * unit - top)
            total = total + jnp.sum(weights, axis=-1, keepdims=True)
            summed = summed + dot(
                weights.astype(BF16), key_s[k * piece : (k + 1) * piece, HDIM:]
            )
        query_s[index] = (summed / total).astype(BF16)
        lane = lax.broadcasted_iota(jnp.int32, (rows, HDIM), 1)
        stat_s[...] = jnp.where(lane == index, top + jnp.log2(total), stat_s[...])
        return carry

    lax.fori_loop(0, SIDE, tile, 0)
    stats = jnp.transpose(stat_s[...])
    for index in range(SIDE):
        outs[index][:rows, :] = query_s[index]
        row = stats[index : index + 1, :]
        high = row.astype(BF16).astype(F32)
        middle = (row - high).astype(BF16).astype(F32)
        low = row - high - middle
        parts = [p[:, at : at + HDIM] for p in (high, middle, low) for at in (0, HDIM)]
        parts.append(jnp.zeros((STAT_ROWS - 6, HDIM), F32))
        outs[index][rows:, :] = jnp.concatenate(parts, axis=0).astype(BF16)


def attend(stale, fresh, asked, early, name):
    rows = 2 * BLOCK
    keys = SIDE * (STALE + 2) * BLOCK
    shape = jax.ShapeDtypeStruct((rows + STAT_ROWS, HDIM), BF16)
    return pl.pallas_call(
        attend_kernel,
        in_specs=[in_hbm()] * (1 + 2 * SIDE) + [anywhere()] * len(early),
        out_specs=[whole()] * SIDE,
        out_shape=[shape] * SIDE,
        scratch_shapes=[
            pltpu.VMEM((keys, 2 * HDIM), BF16),
            pltpu.VMEM((rows, keys), F32),
            pltpu.VMEM((SIDE, rows, HDIM), BF16),
            pltpu.VMEM((rows, HDIM), F32),
            pltpu.SemaphoreType.DMA((1 + 2 * SIDE,)),
        ],
        compiler_params=params(),
        cost_estimate=pl.CostEstimate(
            flops=4 * SIDE * rows * keys * HDIM,
            bytes_accessed=4 * MIB,
            transcendentals=SIDE * rows * keys,
        ),
        name=name,
    )(stale, *fresh, *asked, *early)


def join_kernel(*refs):
    parts, (mine_ref, theirs_ref) = refs[:8], refs[8:]
    rows = 2 * BLOCK
    stats = []
    for part in parts:
        tail = part[rows:, :].astype(F32)
        joined = [jnp.concatenate([tail[i : i + 1], tail[i + 1 : i + 2]], axis=1) for i in (0, 2, 4)]
        stats.append(joined[0] + joined[1] + joined[2])
    stats = jnp.concatenate(stats + [jnp.zeros((HDIM - 2 * SIDE, rows), F32)], axis=0)
    columns = jnp.transpose(stats)
    first = lax.axis_index("branch") == 0
    for head in range(2):
        level = [columns[:, head * SIDE + k : head * SIDE + k + 1] for k in range(SIDE)]
        top = functools.reduce(jnp.maximum, level)
        shares = [jnp.exp2(value - top) for value in level]
        inverse = 1.0 / sum(shares)
        result = sum(
            (shares[k] * inverse) * parts[head * SIDE + k][:rows, :].astype(F32)
            for k in range(SIDE)
        ).astype(BF16)
        at = slice(head * HDIM, (head + 1) * HDIM)
        mine_ref[:, at] = jnp.where(first, result[:BLOCK], result[BLOCK:])
        theirs_ref[:, at] = jnp.where(first, result[BLOCK:], result[:BLOCK])


def join(parts):
    shape = jax.ShapeDtypeStruct((BLOCK, 2 * HDIM), BF16)
    return pl.pallas_call(
        join_kernel,
        in_specs=[whole()] * 8,
        out_specs=[whole()] * 2,
        out_shape=[shape, shape],
        compiler_params=params(4),
        name="join",
    )(*parts)


def stale_kernel(
    blocks_ref, mod_ref, mod_other_ref, own_ref, other_ref, cached_ref, cached_other_ref, out_ref,
    kept_ref, old_ref,
):
    core = lax.axis_index("branch")
    factor = jnp.where(core == 0, 1.0 - GUIDANCE, GUIDANCE)
    width = own_ref.shape[1]
    columns = pl.ds(pl.multiple_of(lax.axis_index("head") * width, width), width)
    gate = factor * mod_ref[2, :, columns]
    gate_other = (1.0 - factor) * mod_other_ref[2, :, columns]
    out_ref[...] = (
        factor * own_ref[...].astype(F32)
        + gate * cached_ref[...].astype(F32)
        + (1.0 - factor) * other_ref[...].astype(F32)
        + gate_other * cached_other_ref[...].astype(F32)
    ).astype(BF16)
    rows = block_rows(jnp.where(core == 0, blocks_ref[0, 0], blocks_ref[0, 1]))
    kept_ref[...] = factor * own_ref[rows, :].astype(F32) + (1.0 - factor) * other_ref[
        rows, :
    ].astype(F32)
    old_ref[...] = out_ref[rows, :]


def stale_rows(blocks, mod, mod_other, own, other, cached, cached_other):
    rows, width = own.shape
    return pl.pallas_call(
        stale_kernel,
        in_specs=[scalars()] + [whole()] * 6,
        out_specs=[whole()] * 3,
        out_shape=[
            jax.ShapeDtypeStruct((rows, width), BF16),
            jax.ShapeDtypeStruct((BLOCK, width), F32),
            jax.ShapeDtypeStruct((BLOCK, width), BF16),
        ],
        compiler_params=params(8),
        name="stale_rows",
    )(blocks, mod, mod_other, own, other, cached, cached_other)


def finish_kernel(counts_ref, parts_ref, kept_ref, old_ref, out_ref):
    total = kept_ref[...]
    for k in range(HEAD):
        total = total + parts_ref[k].astype(F32)
    live = lax.axis_index("branch") < counts_ref[0]
    out_ref[...] = jnp.where(live, total.astype(BF16), old_ref[...])


def finish(counts, parts, kept, old):
    return pl.pallas_call(
        finish_kernel,
        in_specs=[scalars()] + [whole()] * 3,
        out_specs=whole(),
        out_shape=jax.ShapeDtypeStruct(old.shape, BF16),
        compiler_params=params(4),
        name="finish",
    )(counts, parts, kept, old)


def place_kernel(blocks_ref, stale_ref, own_ref, other_ref, out_ref, sent):
    core = lax.axis_index("branch")
    copies = []
    for i, ref in enumerate((own_ref, other_ref)):
        first = core == i
        slot = jnp.where(first, blocks_ref[0, 0], blocks_ref[0, 1])
        copies.append(pltpu.make_async_copy(ref, out_ref.at[block_rows(slot)], sent.at[i]))
    for copy in copies:
        copy.start()
    for copy in copies:
        copy.wait()


def place(blocks, stale, own, other):
    return pl.pallas_call(
        place_kernel,
        in_specs=[scalars(), in_hbm(), whole(), whole()],
        out_specs=in_hbm(),
        out_shape=jax.ShapeDtypeStruct(stale.shape, BF16),
        scratch_shapes=[pltpu.SemaphoreType.DMA((2,))],
        input_output_aliases={1: 0},
        compiler_params=params(2),
        name="place",
    )(blocks, stale, own, other)


def ring(array, shift):
    return lax.ppermute(array, "head", [(i, (i + shift) % HEAD) for i in range(HEAD)])


def swap(array):
    return lax.ppermute(array, "branch", [(0, 1), (1, 0)])


def along(axis, array, shift):
    return lax.ppermute(array, axis, [(i, (i + shift) % SIDE) for i in range(SIDE)])


def local(
    hidden,
    modulation,
    branch_cache,
    k_cache,
    v_cache,
    w_qkv,
    w_mlp_in,
    w_attn_out,
    w_mlp_out,
    q_gain,
    k_gain,
    blocks,
    counts,
):
    tokens, cached = hidden[0], branch_cache[0]
    keys, values = k_cache[0], v_cache[0]
    mod = jnp.transpose(modulation, (1, 0, 2))

    picked, stale_first, stale_second = pick(tokens, keys, values, blocks, counts)
    ups, downs = [picked], [picked]
    for step in range(3):
        ups.append(ring(ups[-1], 1))
        downs.append(ring(downs[-1], -1))
    chunks = ups + [ring(ups[-1], 1)] + downs[:0:-1]

    stale_x = lax.all_gather(stale_first, "x", axis=0, tiled=True)
    stale_y = lax.all_gather(stale_second, "y", axis=0, tiled=True)

    qkv = jnp.transpose(w_qkv, (1, 0, 2))
    qkv_other = swap(qkv)
    mod_other = swap(mod)
    mlp_in_other = swap(w_mlp_in)
    mlp_out_other = swap(w_mlp_out)
    attn_out_other = swap(w_attn_out)
    tokens_other = swap(tokens)
    cached_other = swap(cached)

    message_x, message_y, rows = project(
        blocks,
        counts,
        chunks,
        mod,
        qkv,
        qkv_other,
        q_gain.reshape(1, HDIM),
        k_gain.reshape(1, HDIM),
        keys,
        values,
    )
    fresh_x = [message_x] + [along("x", message_x, k) for k in range(1, SIDE)]
    fresh_y = [message_y] + [along("y", message_y, k) for k in range(1, SIDE)]

    units, units_send = hidden_units(rows, w_mlp_in, mlp_in_other)
    units_other = swap(units_send)
    base = out_product(
        units_out_kernel, F32, "units_out", 14, units, units_other, w_mlp_out, mlp_out_other,
        mod, mod_other,
    )

    part_y = attend(stale_x, fresh_x, fresh_y, [base], "attend_first")
    part_x = attend(stale_y, fresh_y, fresh_x, [part_y[0]], "attend_second")
    parts = [part_y[0]] + [along("y", part_y[k], -k) for k in range(1, SIDE)]
    parts += [part_x[0]] + [along("x", part_x[k], -k) for k in range(1, SIDE)]
    attended, attended_send = join(parts)
    attended_other = swap(attended_send)
    sums = out_product(
        heads_out_kernel, BF16, "heads_out", 10, attended, attended_other, w_attn_out,
        attn_out_other, mod, mod_other, base,
    )
    sums = lax.all_to_all(sums, "head", 0, 0, tiled=True)
    stale, kept, old = stale_rows(
        blocks, mod, mod_other, tokens, tokens_other, cached, cached_other
    )
    final = finish(counts, sums, kept, old)
    return place(blocks, stale, final, swap(final))


def solution(mesh):
    mesh = Mesh(mesh.devices.reshape(2, HEAD, SIDE, SIDE), ("branch", "head", "y", "x"))
    seq = ("y", "x")
    in_specs = (
        P("branch", seq, "head"),
        P("branch", None, None),
        P("branch", seq, "head"),
        P("branch", seq, "head"),
        P("branch", seq, "head"),
        P("branch", None, "head"),
        P("branch", "head"),
        P("head", "branch"),
        P("head", "branch"),
        P(),
        P(),
        P(seq, None),
        P(seq),
    )
    out_specs = P(seq, "head")
    return jax.shard_map(local, mesh=mesh, in_specs=in_specs, out_specs=out_specs, check_vma=False)
```

profile of v0, /device:TPU:1, one launch (start us, length us, event | category | flops | bytes accessed | tf_op | source)
XLA Modules:
  0.0 165.6 jit_solution(1921451162659459300)
XLA Ops:
  7.2 3.6 %pick.1 = (bf16[256,384]{1,0:T(8,128)(2,1)}, bf16[768,256]{1,0:T(8,128)(2,1)}, bf16[768,256]{1,0:T(8,128)(2,1)}) custom-call(s32[1,2]{1,0:T(1,128)} %blocks_ref.7, s32[1]{0:T(128)S(6)} %copy.16.counts_ref, bf16[1024,384]{1,0:T(8,128)(2,1)} %bitcast.8, bf16[1024,256]{1,0:T(8,128)(2,1)} %bitcast.20, bf16[1024,256]{1,0:T(8,128)(2,1)} %bitcast.22), custom_call_target="tpu_custom_call" | custom-call | tf_op jit(solution)/shard_map/pick/pallas_call | solution.py:91
  10.9 3.3 %collective-permute-start.10 = (bf16[3,1536,256]{2,1,0:T(8,128)(2,1)}, bf16[3,1536,256]{2,1,0:T(8,128)(2,1)}, u32[]{:S(2)}, u32[]{:S(2)}) collective-permute-start(bf16[3,1536,256]{2,1,0:T(8,128)(2,1)} %bitcast.18), channel_id=1, source_target_pairs={{0,128},{128,0},{1,129},{129,1},{2,130},{130,2},{3,131},{131,3},{4... | collective-permute-start | bytes 7077896 | tf_op jit(solution)/shard_map/ppermute | solution.py:482
  14.8 3.9 %collective-permute-start.7 = (bf16[256,384]{1,0:T(8,128)(2,1)}, bf16[256,384]{1,0:T(8,128)(2,1)S(1)}, u32[]{:S(2)}, u32[]{:S(2)}) collective-permute-start(bf16[256,384]{1,0:T(8,128)(2,1)} %get-tuple-element.28.refs_0_), channel_id=1, source_target_pairs={{0,112},{16,0},{32,16},{48,32},{64,48},{80,64},{96,80},{112,96},{1... | collective-permute-start | bytes 589832 | tf_op jit(solution)/shard_map/ppermute | solution.py:478
  18.8 5.3 %collective-permute-done.3.refs_1_ = bf16[256,384]{1,0:T(8,128)(2,1)S(1)} collective-permute-done((bf16[256,384]{1,0:T(8,128)(2,1)}, bf16[256,384]{1,0:T(8,128)(2,1)S(1)}, u32[]{:S(2)}, u32[]{:S(2)}) %collective-permute-start.3) | collective-permute-done | bytes 196640 | tf_op jit(solution)/shard_map/ppermute | solution.py:478
  24.0 2.7 %collective-permute-start.8 = (bf16[256,384]{1,0:T(8,128)(2,1)S(1)}, bf16[256,384]{1,0:T(8,128)(2,1)S(1)}, u32[]{:S(2)}, u32[]{:S(2)}) collective-permute-start(bf16[256,384]{1,0:T(8,128)(2,1)S(1)} %collective-permute-done.7.refs_7_), channel_id=1, source_target_pairs={{0,112},{16,0},{32,16},{48,32},{64,48},{80,64},{96,80},{112,96},{1... | collective-permute-start | bytes 589832 | tf_op jit(solution)/shard_map/ppermute | solution.py:478
  26.7 4.3 %collective-permute-done.4.refs_2_ = bf16[256,384]{1,0:T(8,128)(2,1)S(1)} collective-permute-done((bf16[256,384]{1,0:T(8,128)(2,1)S(1)}, bf16[256,384]{1,0:T(8,128)(2,1)S(1)}, u32[]{:S(2)}, u32[]{:S(2)}) %collective-permute-start.4) | collective-permute-done | bytes 196640 | tf_op jit(solution)/shard_map/ppermute | solution.py:478
  31.0 2.7 %collective-permute-start.9 = (bf16[256,384]{1,0:T(8,128)(2,1)S(1)}, bf16[256,384]{1,0:T(8,128)(2,1)S(1)}, u32[]{:S(2)}, u32[]{:S(2)}) collective-permute-start(bf16[256,384]{1,0:T(8,128)(2,1)S(1)} %collective-permute-done.8.refs_6_), channel_id=1, source_target_pairs={{0,112},{16,0},{32,16},{48,32},{64,48},{80,64},{96,80},{112,96},{1... | collective-permute-start | bytes 589832 | tf_op jit(solution)/shard_map/ppermute | solution.py:478
  33.7 3.5 %collective-permute-done.5.refs_3_ = bf16[256,384]{1,0:T(8,128)(2,1)S(1)} collective-permute-done((bf16[256,384]{1,0:T(8,128)(2,1)S(1)}, bf16[256,384]{1,0:T(8,128)(2,1)S(1)}, u32[]{:S(2)}, u32[]{:S(2)}) %collective-permute-start.5) | collective-permute-done | bytes 196640 | tf_op jit(solution)/shard_map/ppermute | solution.py:478
  37.2 6.1 %collective-permute-done.6.refs_4_ = bf16[256,384]{1,0:T(8,128)(2,1)S(1)} collective-permute-done((bf16[256,384]{1,0:T(8,128)(2,1)S(1)}, bf16[256,384]{1,0:T(8,128)(2,1)S(1)}, u32[]{:S(2)}, u32[]{:S(2)}) %collective-permute-start.6) | collective-permute-done | bytes 196640 | tf_op jit(solution)/shard_map/ppermute | solution.py:478
  44.0 6.8 %project.1 = (bf16[256,384]{1,0:T(8,128)(2,1)}, bf16[256,384]{1,0:T(8,128)(2,1)}, bf16[256,3072]{1,0:T(8,128)(2,1)}) custom-call(s32[1,2]{1,0:T(1,128)} %blocks_ref.7, s32[1]{0:T(128)S(6)} %copy.16.counts_ref, bf16[256,384]{1,0:T(8,128)(2,1)} %get-tuple-element.28.refs_0_, bf16[256,384]{1,0:T(8,128)(2,1)} %copy-done.14, bf16[256,384]{1,0:T(8,128)(2,1)} %copy-done.16, ...), custom_call_target="tpu_custom_call" | custom-call | flops 1207959552 | bytes 8388608 | tf_op jit(solution)/shard_map/project/pallas_call | solution.py:169
  50.8 1.4 copy-done.5
  52.2 1.5 hidden_units.1
  53.7 3.2 %collective-permute-start.18 = (bf16[128,768]{1,0:T(8,128)(2,1)S(1)}, bf16[128,768]{1,0:T(8,128)(2,1)S(1)}, u32[]{:S(2)}, u32[]{:S(2)}) collective-permute-start(bf16[128,768]{1,0:T(8,128)(2,1)S(1)} %get-tuple-element.33), channel_id=1, source_target_pairs={{0,128},{128,0},{1,129},{129,1},{2,130},{130,2},{3,131},{131,3},{4... | collective-permute-start | bytes 589832 | tf_op jit(solution)/shard_map/ppermute | solution.py:482
  56.9 1.2 collective-permute-start.11
  58.1 2.6 %collective-permute-start.12 = (bf16[256,384]{1,0:T(8,128)(2,1)S(1)}, bf16[256,384]{1,0:T(8,128)(2,1)S(1)}, u32[]{:S(2)}, u32[]{:S(2)}) collective-permute-start(bf16[256,384]{1,0:T(8,128)(2,1)S(1)} %copy-done.21), channel_id=1, source_target_pairs={{0,2},{1,3},{2,0},{3,1},{4,6},{5,7},{6,4},{7,5},{8,10},{9,11},{10,... | collective-permute-start | bytes 589832 | tf_op jit(solution)/shard_map/ppermute | solution.py:486
  63.5 1.3 collective-permute-start.14
  64.8 2.6 %collective-permute-start.15 = (bf16[256,384]{1,0:T(8,128)(2,1)}, bf16[256,384]{1,0:T(8,128)(2,1)S(1)}, u32[]{:S(2)}, u32[]{:S(2)}) collective-permute-start(bf16[256,384]{1,0:T(8,128)(2,1)} %get-tuple-element.30.refs_5_.refs_1_), channel_id=1, source_target_pairs={{0,8},{4,12},{8,0},{12,4},{1,9},{5,13},{9,1},{13,5},{2,10},{6,14},... | collective-permute-start | bytes 589832 | tf_op jit(solution)/shard_map/ppermute | solution.py:486
  68.5 1.2 collective-permute-done.12.refs_3_.refs_7_
  70.8 3.1 %units_out.1.refs_9_.base_ref = f32[8,128,384]{2,1,0:T(8,128)S(1)} custom-call(bf16[128,768]{1,0:T(8,128)(2,1)S(1)} %get-tuple-element.32.mine_ref, bf16[128,768]{1,0:T(8,128)(2,1)S(1)} %collective-permute-done.18.theirs_ref, bf16[768,1536]{1,0:T(8,128)(2,1)S(1)} %copy-done.4, bf16[768,1536]{1,0:T(8,128)(2,1)} %collective-permute-done.19.other_ref, ...), custom_call_target="tpu_custom_call" | custom-call | flops 1207959552 | bytes 6291456 | tf_op jit(solution)/shard_map/units_out/pallas_call | solution.py:256
  75.8 7.3 %collective-permute-done.15.refs_7_.refs_3_ = bf16[256,384]{1,0:T(8,128)(2,1)S(1)} collective-permute-done((bf16[256,384]{1,0:T(8,128)(2,1)}, bf16[256,384]{1,0:T(8,128)(2,1)S(1)}, u32[]{:S(2)}, u32[]{:S(2)}) %collective-permute-start.15) | collective-permute-done | bytes 196640 | tf_op jit(solution)/shard_map/ppermute | solution.py:486
  84.4 10.6 %attend_first.1 = (bf16[272,128]{1,0:T(8,128)(2,1)}, bf16[272,128]{1,0:T(8,128)(2,1)}, bf16[272,128]{1,0:T(8,128)(2,1)}, bf16[272,128]{1,0:T(8,128)(2,1)}) custom-call(bf16[3072,256]{1,0:T(8,128)(2,1)} %all-gather.3.cloned.1.call-done.refs_0_, bf16[256,384]{1,0:T(8,128)(2,1)} %get-tuple-element.29.refs_1_.refs_5_, bf16[256,384]{1,0:T(8,128)(2,1)} %copy-done.22, ...), custom_call_target="tpu_custom_call" | custom-call | flops 2147483648 | bytes 4194304 | tf_op jit(solution)/shard_map/attend_first/pallas_call | solution.py:334
  95.1 10.7 %attend_second.1 = (bf16[272,128]{1,0:T(8,128)(2,1)}, bf16[272,128]{1,0:T(8,128)(2,1)}, bf16[272,128]{1,0:T(8,128)(2,1)}, bf16[272,128]{1,0:T(8,128)(2,1)}) custom-call(bf16[3072,256]{1,0:T(8,128)(2,1)} %all-gather.5.cloned.1.call-done.refs_0_, bf16[256,384]{1,0:T(8,128)(2,1)} %get-tuple-element.30.refs_5_.refs_1_, bf16[256,384]{1,0:T(8,128)(2,1)} %copy-done.25, ...), custom_call_target="tpu_custom_call" | custom-call | flops 2147483648 | bytes 4194304 | tf_op jit(solution)/shard_map/attend_second/pallas_call | solution.py:334
  105.8 2.4 %collective-permute-start.23 = (bf16[272,128]{1,0:T(8,128)(2,1)}, bf16[272,128]{1,0:T(8,128)(2,1)S(1)}, u32[]{:S(2)}, u32[]{:S(2)}) collective-permute-start(bf16[272,128]{1,0:T(8,128)(2,1)} %get-tuple-element.40), channel_id=1, source_target_pairs={{0,3},{1,0},{2,1},{3,2},{4,7},{5,4},{6,5},{7,6},{8,11},{9,8},{10,9... | collective-permute-start | bytes 208904 | tf_op jit(solution)/shard_map/ppermute | solution.py:486
  110.5 2.6 %collective-permute-done.24.refs_6_ = bf16[272,128]{1,0:T(8,128)(2,1)S(1)} collective-permute-done((bf16[272,128]{1,0:T(8,128)(2,1)}, bf16[272,128]{1,0:T(8,128)(2,1)S(1)}, u32[]{:S(2)}, u32[]{:S(2)}) %collective-permute-start.24) | collective-permute-done | bytes 69664 | tf_op jit(solution)/shard_map/ppermute | solution.py:486
  114.9 2.8 %collective-permute-done.22.refs_3_ = bf16[272,128]{1,0:T(8,128)(2,1)S(1)} collective-permute-done((bf16[272,128]{1,0:T(8,128)(2,1)S(1)}, bf16[272,128]{1,0:T(8,128)(2,1)S(1)}, u32[]{:S(2)}, u32[]{:S(2)}) %collective-permute-start.22) | collective-permute-done | bytes 69664 | tf_op jit(solution)/shard_map/ppermute | solution.py:486
  119.7 3.3 %collective-permute-start.26 = (bf16[128,256]{1,0:T(8,128)(2,1)S(1)}, bf16[128,256]{1,0:T(8,128)(2,1)S(1)}, u32[]{:S(2)}, u32[]{:S(2)}) collective-permute-start(bf16[128,256]{1,0:T(8,128)(2,1)S(1)} %get-tuple-element.44), channel_id=1, source_target_pairs={{0,128},{128,0},{1,129},{129,1},{2,130},{130,2},{3,131},{131,3},{4... | collective-permute-start | bytes 196616 | tf_op jit(solution)/shard_map/ppermute | solution.py:482
  125.1 1.5 heads_out.1
  126.6 5.7 %all-to-all-start = ((bf16[8,128,384]{2,1,0:T(8,128)(2,1)}), bf16[8,128,384]{2,1,0:T(8,128)(2,1)S(1)}, u32[]{:S(2)}, u32[]{:S(2)}) async-start(bf16[8,128,384]{2,1,0:T(8,128)(2,1)} %heads_out.1), calls=%async_computation | async-start | bytes 1572864 | tf_op jit(solution)/shard_map/all_to_all | solution.py:559
  133.1 1.8 %collective-permute-done.1.other_ref = bf16[1024,384]{1,0:T(8,128)(2,1)S(1)} collective-permute-done((bf16[1024,384]{1,0:T(8,128)(2,1)S(1)}, bf16[1024,384]{1,0:T(8,128)(2,1)S(1)}, u32[]{:S(2)}, u32[]{:S(2)}) %collective-permute-start.1) | collective-permute-done | bytes 786464 | tf_op jit(solution)/shard_map/ppermute | solution.py:482
  136.0 2.7 %stale_rows.1 = (bf16[1024,384]{1,0:T(8,128)(2,1)}, f32[128,384]{1,0:T(8,128)S(1)}, bf16[128,384]{1,0:T(8,128)(2,1)S(1)}) custom-call(s32[1,2]{1,0:T(1,128)S(1)} %copy-done.13, f32[3,1,3072]{2,1,0:T(1,128)S(1)} %bitcast.17, f32[3,1,3072]{2,1,0:T(1,128)S(1)} %collective-permute-done.mod_other_ref, bf16[1024,384]{1,0:T(8,128)(2,1)S(1)} %bitcast.10, ...), custom_call_target="tpu_custom_call" | custom-call | tf_op jit(solution)/shard_map/stale_rows/pallas_call | solution.py:418
  138.8 17.1 %all-to-all-done.parts_ref = bf16[8,128,384]{2,1,0:T(8,128)(2,1)S(1)} async-done(((bf16[8,128,384]{2,1,0:T(8,128)(2,1)}), bf16[8,128,384]{2,1,0:T(8,128)(2,1)S(1)}, u32[]{:S(2)}, u32[]{:S(2)}) %all-to-all-start) | async-done | bytes 786464 | tf_op jit(solution)/shard_map/all_to_all | solution.py:559
  157.5 1.2 place.1
  (107 shorter events, 21.3 us)
Async XLA Ops:
  6.5 68.6 %all-gather.3.cloned.1.call-start = ((), (), s32[]{:S(2)}) async-start(), calls=%async_computation.1 | async-start | bytes 1966080 | tf_op jit(solution)/shard_map/all_gather | solution.py:515
  10.8 84.3 %all-gather.5.cloned.1.call-start = ((), (), s32[]{:S(2)}) async-start(), calls=%async_computation.2 | async-start | bytes 1966080 | tf_op jit(solution)/shard_map/all_gather | solution.py:516
  10.9 32.4 %collective-permute-start.10 = (bf16[3,1536,256]{2,1,0:T(8,128)(2,1)}, bf16[3,1536,256]{2,1,0:T(8,128)(2,1)}, u32[]{:S(2)}, u32[]{:S(2)}) collective-permute-start(bf16[3,1536,256]{2,1,0:T(8,128)(2,1)} %bitcast.18), channel_id=1, source_target_pairs={{0,128},{128,0},{1,129},{129,1},{2,130},{130,2},{3,131},{131,3},{4... | collective-permute-start | bytes 7077896 | tf_op jit(solution)/shard_map/ppermute | solution.py:482
  14.2 36.6 %collective-permute-start.17 = (bf16[1536,768]{1,0:T(8,128)(2,1)}, bf16[1536,768]{1,0:T(8,128)(2,1)S(1)}, u32[]{:S(2)}, u32[]{:S(2)}) collective-permute-start(bf16[1536,768]{1,0:T(8,128)(2,1)} %own_ref.3), channel_id=1, source_target_pairs={{0,128},{128,0},{1,129},{129,1},{2,130},{130,2},{3,131},{131,3},{4... | collective-permute-start | bytes 7077896 | tf_op jit(solution)/shard_map/ppermute | solution.py:482
  14.3 49.2 %collective-permute-start.19 = (bf16[768,1536]{1,0:T(8,128)(2,1)}, bf16[768,1536]{1,0:T(8,128)(2,1)}, u32[]{:S(2)}, u32[]{:S(2)}) collective-permute-start(bf16[768,1536]{1,0:T(8,128)(2,1)} %own_ref.4), channel_id=1, source_target_pairs={{0,128},{128,0},{1,129},{129,1},{2,130},{130,2},{3,131},{131,3},{4... | collective-permute-start | bytes 7077896 | tf_op jit(solution)/shard_map/ppermute | solution.py:482
  14.7 9.3 %collective-permute-start.3 = (bf16[256,384]{1,0:T(8,128)(2,1)}, bf16[256,384]{1,0:T(8,128)(2,1)S(1)}, u32[]{:S(2)}, u32[]{:S(2)}) collective-permute-start(bf16[256,384]{1,0:T(8,128)(2,1)} %get-tuple-element.28.refs_0_), channel_id=1, source_target_pairs={{0,16},{16,32},{32,48},{48,64},{64,80},{80,96},{96,112},{112,0},{1... | collective-permute-start | bytes 589832 | tf_op jit(solution)/shard_map/ppermute | solution.py:478
  14.8 9.2 %collective-permute-start.7 = (bf16[256,384]{1,0:T(8,128)(2,1)}, bf16[256,384]{1,0:T(8,128)(2,1)S(1)}, u32[]{:S(2)}, u32[]{:S(2)}) collective-permute-start(bf16[256,384]{1,0:T(8,128)(2,1)} %get-tuple-element.28.refs_0_), channel_id=1, source_target_pairs={{0,112},{16,0},{32,16},{48,32},{64,48},{80,64},{96,80},{112,96},{1... | collective-permute-start | bytes 589832 | tf_op jit(solution)/shard_map/ppermute | solution.py:478
  24.0 7.0 %collective-permute-start.4 = (bf16[256,384]{1,0:T(8,128)(2,1)S(1)}, bf16[256,384]{1,0:T(8,128)(2,1)S(1)}, u32[]{:S(2)}, u32[]{:S(2)}) collective-permute-start(bf16[256,384]{1,0:T(8,128)(2,1)S(1)} %collective-permute-done.3.refs_1_), channel_id=1, source_target_pairs={{0,16},{16,32},{32,48},{48,64},{64,80},{80,96},{96,112},{112,0},{1... | collective-permute-start | bytes 589832 | tf_op jit(solution)/shard_map/ppermute | solution.py:478
  24.0 7.0 %collective-permute-start.8 = (bf16[256,384]{1,0:T(8,128)(2,1)S(1)}, bf16[256,384]{1,0:T(8,128)(2,1)S(1)}, u32[]{:S(2)}, u32[]{:S(2)}) collective-permute-start(bf16[256,384]{1,0:T(8,128)(2,1)S(1)} %collective-permute-done.7.refs_7_), channel_id=1, source_target_pairs={{0,112},{16,0},{32,16},{48,32},{64,48},{80,64},{96,80},{112,96},{1... | collective-permute-start | bytes 589832 | tf_op jit(solution)/shard_map/ppermute | solution.py:478
  31.0 6.2 %collective-permute-start.5 = (bf16[256,384]{1,0:T(8,128)(2,1)S(1)}, bf16[256,384]{1,0:T(8,128)(2,1)S(1)}, u32[]{:S(2)}, u32[]{:S(2)}) collective-permute-start(bf16[256,384]{1,0:T(8,128)(2,1)S(1)} %collective-permute-done.4.refs_2_), channel_id=1, source_target_pairs={{0,16},{16,32},{32,48},{48,64},{64,80},{80,96},{96,112},{112,0},{1... | collective-permute-start | bytes 589832 | tf_op jit(solution)/shard_map/ppermute | solution.py:478
  31.0 6.1 %collective-permute-start.9 = (bf16[256,384]{1,0:T(8,128)(2,1)S(1)}, bf16[256,384]{1,0:T(8,128)(2,1)S(1)}, u32[]{:S(2)}, u32[]{:S(2)}) collective-permute-start(bf16[256,384]{1,0:T(8,128)(2,1)S(1)} %collective-permute-done.8.refs_6_), channel_id=1, source_target_pairs={{0,112},{16,0},{32,16},{48,32},{64,48},{80,64},{96,80},{112,96},{1... | collective-permute-start | bytes 589832 | tf_op jit(solution)/shard_map/ppermute | solution.py:478
  37.2 6.1 %collective-permute-start.6 = (bf16[256,384]{1,0:T(8,128)(2,1)S(1)}, bf16[256,384]{1,0:T(8,128)(2,1)S(1)}, u32[]{:S(2)}, u32[]{:S(2)}) collective-permute-start(bf16[256,384]{1,0:T(8,128)(2,1)S(1)} %collective-permute-done.5.refs_3_), channel_id=1, source_target_pairs={{0,16},{16,32},{32,48},{48,64},{64,80},{80,96},{96,112},{112,0},{1... | collective-permute-start | bytes 589832 | tf_op jit(solution)/shard_map/ppermute | solution.py:478
  53.7 11.0 %collective-permute-start.18 = (bf16[128,768]{1,0:T(8,128)(2,1)S(1)}, bf16[128,768]{1,0:T(8,128)(2,1)S(1)}, u32[]{:S(2)}, u32[]{:S(2)}) collective-permute-start(bf16[128,768]{1,0:T(8,128)(2,1)S(1)} %get-tuple-element.33), channel_id=1, source_target_pairs={{0,128},{128,0},{1,129},{129,1},{2,130},{130,2},{3,131},{131,3},{4... | collective-permute-start | bytes 589832 | tf_op jit(solution)/shard_map/ppermute | solution.py:482
  56.9 10.4 %collective-permute-start.11 = (bf16[256,384]{1,0:T(8,128)(2,1)S(1)}, bf16[256,384]{1,0:T(8,128)(2,1)S(1)}, u32[]{:S(2)}, u32[]{:S(2)}) collective-permute-start(bf16[256,384]{1,0:T(8,128)(2,1)S(1)} %copy-done.21), channel_id=1, source_target_pairs={{0,1},{1,2},{2,3},{3,0},{4,5},{5,6},{6,7},{7,4},{8,9},{9,10},{10,1... | collective-permute-start | bytes 589832 | tf_op jit(solution)/shard_map/ppermute | solution.py:486
  58.1 11.5 %collective-permute-start.12 = (bf16[256,384]{1,0:T(8,128)(2,1)S(1)}, bf16[256,384]{1,0:T(8,128)(2,1)S(1)}, u32[]{:S(2)}, u32[]{:S(2)}) collective-permute-start(bf16[256,384]{1,0:T(8,128)(2,1)S(1)} %copy-done.21), channel_id=1, source_target_pairs={{0,2},{1,3},{2,0},{3,1},{4,6},{5,7},{6,4},{7,5},{8,10},{9,11},{10,... | collective-permute-start | bytes 589832 | tf_op jit(solution)/shard_map/ppermute | solution.py:486
  60.7 1.7 %collective-permute-start = (f32[3,1,3072]{2,1,0:T(1,128)S(1)}, f32[3,1,3072]{2,1,0:T(1,128)S(1)}, u32[]{:S(2)}, u32[]{:S(2)}) collective-permute-start(f32[3,1,3072]{2,1,0:T(1,128)S(1)} %bitcast.14), channel_id=1, source_target_pairs={{0,128},{128,0},{1,129},{129,1},{2,130},{130,2},{3,131},{131,3},{4... | collective-permute-start | bytes 110600 | tf_op jit(solution)/shard_map/ppermute | solution.py:482
  62.4 12.7 %collective-permute-start.13 = (bf16[256,384]{1,0:T(8,128)(2,1)S(1)}, bf16[256,384]{1,0:T(8,128)(2,1)S(1)}, u32[]{:S(2)}, u32[]{:S(2)}) collective-permute-start(bf16[256,384]{1,0:T(8,128)(2,1)S(1)} %copy-done.21), channel_id=1, source_target_pairs={{0,3},{1,0},{2,1},{3,2},{4,7},{5,4},{6,5},{7,6},{8,11},{9,8},{10,9... | collective-permute-start | bytes 589832 | tf_op jit(solution)/shard_map/ppermute | solution.py:486
  63.5 12.4 %collective-permute-start.14 = (bf16[256,384]{1,0:T(8,128)(2,1)}, bf16[256,384]{1,0:T(8,128)(2,1)S(1)}, u32[]{:S(2)}, u32[]{:S(2)}) collective-permute-start(bf16[256,384]{1,0:T(8,128)(2,1)} %get-tuple-element.30.refs_5_.refs_1_), channel_id=1, source_target_pairs={{0,4},{4,8},{8,12},{12,0},{1,5},{5,9},{9,13},{13,1},{2,6},{6,10},{... | collective-permute-start | bytes 589832 | tf_op jit(solution)/shard_map/ppermute | solution.py:486
  64.8 18.3 %collective-permute-start.15 = (bf16[256,384]{1,0:T(8,128)(2,1)}, bf16[256,384]{1,0:T(8,128)(2,1)S(1)}, u32[]{:S(2)}, u32[]{:S(2)}) collective-permute-start(bf16[256,384]{1,0:T(8,128)(2,1)} %get-tuple-element.30.refs_5_.refs_1_), channel_id=1, source_target_pairs={{0,8},{4,12},{8,0},{12,4},{1,9},{5,13},{9,1},{13,5},{2,10},{6,14},... | collective-permute-start | bytes 589832 | tf_op jit(solution)/shard_map/ppermute | solution.py:486
  67.4 15.7 %collective-permute-start.16 = (bf16[256,384]{1,0:T(8,128)(2,1)}, bf16[256,384]{1,0:T(8,128)(2,1)S(1)}, u32[]{:S(2)}, u32[]{:S(2)}) collective-permute-start(bf16[256,384]{1,0:T(8,128)(2,1)} %get-tuple-element.30.refs_5_.refs_1_), channel_id=1, source_target_pairs={{0,12},{4,0},{8,4},{12,8},{1,13},{5,1},{9,5},{13,9},{2,14},{6,2},{... | collective-permute-start | bytes 589832 | tf_op jit(solution)/shard_map/ppermute | solution.py:486
  69.7 53.4 %collective-permute-start.27 = (bf16[256,1536]{1,0:T(8,128)(2,1)S(1)}, bf16[256,1536]{1,0:T(8,128)(2,1)S(1)}, u32[]{:S(2)}, u32[]{:S(2)}) collective-permute-start(bf16[256,1536]{1,0:T(8,128)(2,1)S(1)} %copy-done.7), channel_id=1, source_target_pairs={{0,128},{128,0},{1,129},{129,1},{2,130},{130,2},{3,131},{131,3},{4... | collective-permute-start | bytes 2359304 | tf_op jit(solution)/shard_map/ppermute | solution.py:482
  105.8 4.1 %collective-permute-start.23 = (bf16[272,128]{1,0:T(8,128)(2,1)}, bf16[272,128]{1,0:T(8,128)(2,1)S(1)}, u32[]{:S(2)}, u32[]{:S(2)}) collective-permute-start(bf16[272,128]{1,0:T(8,128)(2,1)} %get-tuple-element.40), channel_id=1, source_target_pairs={{0,3},{1,0},{2,1},{3,2},{4,7},{5,4},{6,5},{7,6},{8,11},{9,8},{10,9... | collective-permute-start | bytes 208904 | tf_op jit(solution)/shard_map/ppermute | solution.py:486
  108.2 4.9 %collective-permute-start.24 = (bf16[272,128]{1,0:T(8,128)(2,1)}, bf16[272,128]{1,0:T(8,128)(2,1)S(1)}, u32[]{:S(2)}, u32[]{:S(2)}) collective-permute-start(bf16[272,128]{1,0:T(8,128)(2,1)} %get-tuple-element.41), channel_id=1, source_target_pairs={{0,2},{1,3},{2,0},{3,1},{4,6},{5,7},{6,4},{7,5},{8,10},{9,11},{10,... | collective-permute-start | bytes 208904 | tf_op jit(solution)/shard_map/ppermute | solution.py:486
  108.9 4.9 %collective-permute-start.25 = (bf16[272,128]{1,0:T(8,128)(2,1)}, bf16[272,128]{1,0:T(8,128)(2,1)S(1)}, u32[]{:S(2)}, u32[]{:S(2)}) collective-permute-start(bf16[272,128]{1,0:T(8,128)(2,1)} %get-tuple-element.42), channel_id=1, source_target_pairs={{0,1},{1,2},{2,3},{3,0},{4,5},{5,6},{6,7},{7,4},{8,9},{9,10},{10,1... | collective-permute-start | bytes 208904 | tf_op jit(solution)/shard_map/ppermute | solution.py:486
  109.2 4.6 %collective-permute-start.20 = (bf16[272,128]{1,0:T(8,128)(2,1)S(1)}, bf16[272,128]{1,0:T(8,128)(2,1)S(1)}, u32[]{:S(2)}, u32[]{:S(2)}) collective-permute-start(bf16[272,128]{1,0:T(8,128)(2,1)S(1)} %copy-done.30), channel_id=1, source_target_pairs={{0,12},{4,0},{8,4},{12,8},{1,13},{5,1},{9,5},{13,9},{2,14},{6,2},{... | collective-permute-start | bytes 208904 | tf_op jit(solution)/shard_map/ppermute | solution.py:486
  109.9 5.0 %collective-permute-start.21 = (bf16[272,128]{1,0:T(8,128)(2,1)S(1)}, bf16[272,128]{1,0:T(8,128)(2,1)S(1)}, u32[]{:S(2)}, u32[]{:S(2)}) collective-permute-start(bf16[272,128]{1,0:T(8,128)(2,1)S(1)} %copy-done.29), channel_id=1, source_target_pairs={{0,8},{4,12},{8,0},{12,4},{1,9},{5,13},{9,1},{13,5},{2,10},{6,14},... | collective-permute-start | bytes 208904 | tf_op jit(solution)/shard_map/ppermute | solution.py:486
  113.1 4.6 %collective-permute-start.22 = (bf16[272,128]{1,0:T(8,128)(2,1)S(1)}, bf16[272,128]{1,0:T(8,128)(2,1)S(1)}, u32[]{:S(2)}, u32[]{:S(2)}) collective-permute-start(bf16[272,128]{1,0:T(8,128)(2,1)S(1)} %copy-done.28), channel_id=1, source_target_pairs={{0,4},{4,8},{8,12},{12,0},{1,5},{5,9},{9,13},{13,1},{2,6},{6,10},{... | collective-permute-start | bytes 208904 | tf_op jit(solution)/shard_map/ppermute | solution.py:486
  119.7 4.2 %collective-permute-start.26 = (bf16[128,256]{1,0:T(8,128)(2,1)S(1)}, bf16[128,256]{1,0:T(8,128)(2,1)S(1)}, u32[]{:S(2)}, u32[]{:S(2)}) collective-permute-start(bf16[128,256]{1,0:T(8,128)(2,1)S(1)} %get-tuple-element.44), channel_id=1, source_target_pairs={{0,128},{128,0},{1,129},{129,1},{2,130},{130,2},{3,131},{131,3},{4... | collective-permute-start | bytes 196616 | tf_op jit(solution)/shard_map/ppermute | solution.py:482
  126.6 29.2 %all-to-all-start = ((bf16[8,128,384]{2,1,0:T(8,128)(2,1)}), bf16[8,128,384]{2,1,0:T(8,128)(2,1)S(1)}, u32[]{:S(2)}, u32[]{:S(2)}) async-start(bf16[8,128,384]{2,1,0:T(8,128)(2,1)} %heads_out.1), calls=%async_computation | async-start | bytes 1572864 | tf_op jit(solution)/shard_map/all_to_all | solution.py:559
  132.3 2.6 %collective-permute-start.1 = (bf16[1024,384]{1,0:T(8,128)(2,1)S(1)}, bf16[1024,384]{1,0:T(8,128)(2,1)S(1)}, u32[]{:S(2)}, u32[]{:S(2)}) collective-permute-start(bf16[1024,384]{1,0:T(8,128)(2,1)S(1)} %bitcast.9), channel_id=1, source_target_pairs={{0,128},{128,0},{1,129},{129,1},{2,130},{130,2},{3,131},{131,3},{4... | collective-permute-start | bytes 2359304 | tf_op jit(solution)/shard_map/ppermute | solution.py:482
  133.0 3.0 %collective-permute-start.2 = (bf16[1024,384]{1,0:T(8,128)(2,1)S(1)}, bf16[1024,384]{1,0:T(8,128)(2,1)S(1)}, u32[]{:S(2)}, u32[]{:S(2)}) collective-permute-start(bf16[1024,384]{1,0:T(8,128)(2,1)S(1)} %bitcast.11), channel_id=1, source_target_pairs={{0,128},{128,0},{1,129},{129,1},{2,130},{130,2},{3,131},{131,3},{4... | collective-permute-start | bytes 2359304 | tf_op jit(solution)/shard_map/ppermute | solution.py:482
  156.0 1.5 collective-permute-start.28
  (31 other events, 289.5 us)
Sparse Core Ops, SparseCore 0:
  10.9 32.8 all-gather.2
  45.6 34.5 all-gather.4
where the time goes:
time: 166 us
  waiting for transfers between devices  58.1 us (35%)
  Pallas kernels  43 us (26%)
  starting transfers between devices  42.6 us (26%)
  between operations  14.4 us (9%)
  local copies, waits for them, and re-layouts  7.52 us (5%)
    pallas_call x2, Pallas kernels, attend(): pl.pallas_call(attend_kernel, in_specs=[in_hbm()] * (1 + 2 * SIDE) + [any...  21.3 us
    ppermute x7, waiting for transfers between devices, ring(): lax.ppermute(array, 'head', [(i, (i + shift) % HEAD) for i in range(HEAD)])  19.2 us
    all_to_all x1, waiting for transfers between devices, local(): sums = lax.all_to_all(sums, 'head', 0, 0, tiled=True)  17.1 us
    ppermute x12, waiting for transfers between devices, along(): lax.ppermute(array, axis, [(i, (i + shift) % SIDE) for i in range(SIDE)])  17 us
    ppermute x12, starting transfers between devices, along(): lax.ppermute(array, axis, [(i, (i + shift) % SIDE) for i in range(SIDE)])  13.8 us
    ppermute x10, starting transfers between devices, swap(): return lax.ppermute(array, 'branch', [(0, 1), (1, 0)])  13.7 us
    ppermute x7, starting transfers between devices, ring(): lax.ppermute(array, 'head', [(i, (i + shift) % HEAD) for i in range(HEAD)])  9.35 us
    unnamed x62, local copies, waits for them, and re-layouts  7.52 us
  transfers between devices with their start and end apart: 32, of which 17 were waited for; matrix products, arithmetic and copies ran while one was open for 0% of the time, Pallas kernels for 22%

commit v1 on v0

--- a/solution.py
+++ b/solution.py
@@ -106,8 +106,8 @@
 def project_kernel(blocks_ref, counts_ref, *refs):
     sources = refs[: HEAD + 5]
     keys_ref, values_ref = refs[HEAD + 5 : HEAD + 7]
-    x_ref, y_ref, rows_ref = refs[HEAD + 7 : HEAD + 10]
-    chunk_s, mod_ref, own_ref, other_ref, q_gain_ref, k_gain_ref, old_s, arrived = refs[HEAD + 10 :]
+    x_ref, y_ref, asked_ref, rows_ref = refs[HEAD + 7 : HEAD + 11]
+    chunk_s, mod_ref, own_ref, other_ref, q_gain_ref, k_gain_ref, old_s, arrived = refs[HEAD + 11 :]
     core = lax.axis_index("branch")
     z = lax.axis_index("head")
     old = block_rows(blocks_ref[0, 1])
@@ -149,9 +149,10 @@
         return (values * lax.rsqrt(power + EPSILON) * gain_ref[...]).astype(BF16)
 
     live = counts_ref[0] > 1
-    for head, fresh_ref, query_ref in ((0, x_ref, y_ref), (1, y_ref, x_ref)):
+    asked_ref[...] = norm(query[:, :HDIM], q_gain_ref)
+    x_ref[:, 2 * HDIM :] = norm(query[:, HDIM:], q_gain_ref)
+    for head, fresh_ref in ((0, x_ref), (1, y_ref)):
         at = head * HDIM
-        query_ref[:, 2 * HDIM :] = norm(query[:, at : at + HDIM], q_gain_ref)
         new_key = norm(key[:, at : at + HDIM], k_gain_ref)
         new_value = value[:, at : at + HDIM].astype(BF16)
         fresh_ref[:BLOCK, :HDIM] = new_key[:BLOCK]
@@ -169,10 +170,11 @@
     return pl.pallas_call(
         project_kernel,
         in_specs=[scalars()] * 2 + [in_hbm()] * len(sources),
-        out_specs=[whole()] * 3,
+        out_specs=[whole()] * 4,
         out_shape=[
             jax.ShapeDtypeStruct((rows, 3 * HDIM), BF16),
-            jax.ShapeDtypeStruct((rows, 3 * HDIM), BF16),
+            jax.ShapeDtypeStruct((rows, 2 * HDIM), BF16),
+            jax.ShapeDtypeStruct((rows, HDIM), BF16),
             jax.ShapeDtypeStruct((rows, full), BF16),
         ],
         scratch_shapes=[
@@ -279,7 +281,9 @@
     piece = keys // tiles
     unit = LOG2E * HDIM**-0.5
     old = stale_ref.shape[0]
-    pairs = [(asked[k].at[:, pl.ds(2 * HDIM, HDIM)], query_s.at[k]) for k in range(SIDE)]
+    pairs = [
+        (ref.at[:, pl.ds(ref.shape[1] - HDIM, HDIM)], query_s.at[k]) for k, ref in enumerate(asked)
+    ]
     pairs += [
         (fresh[k].at[:, pl.ds(0, 2 * HDIM)], key_s.at[pl.ds(old + k * rows, rows)])
         for k in range(SIDE)
@@ -524,7 +528,7 @@
     tokens_other = swap(tokens)
     cached_other = swap(cached)
 
-    message_x, message_y, rows = project(
+    message_x, message_y, asked, rows = project(
         blocks,
         counts,
         chunks,
@@ -537,6 +541,7 @@
         values,
     )
     fresh_x = [message_x] + [along("x", message_x, k) for k in range(1, SIDE)]
+    asked_y = [asked] + [along("y", asked, k) for k in range(1, SIDE)]
     fresh_y = [message_y] + [along("y", message_y, k) for k in range(1, SIDE)]
 
     units, units_send = hidden_units(rows, w_mlp_in, mlp_in_other)
@@ -546,7 +551,7 @@
         mod, mod_other,
     )
 
-    part_y = attend(stale_x, fresh_x, fresh_y, [base], "attend_first")
+    part_y = attend(stale_x, fresh_x, asked_y, [base], "attend_first")
     part_x = attend(stale_y, fresh_y, fresh_x, [part_y[0]], "attend_second")
     parts = [part_y[0]] + [along("y", part_y[k], -k) for k in range(1, SIDE)]
     parts += [part_x[0]] + [along("x", part_x[k], -k) for k in range(1, SIDE)]

time: 166 us -> 159 us (0.958)
  waiting for transfers between devices: 58.1 us -> 46.9 us
  starting transfers between devices: 42.6 us -> 46.6 us
    ppermute x12 -> x15, waiting for transfers between devices: 17 us -> 5.78 us  [along(): lax.ppermute(array, axis, [(i, (i + shift) % SIDE) for i in range(SIDE)])]
    ppermute x12 -> x15, starting transfers between devices: 13.8 us -> 18.6 us  [along(): lax.ppermute(array, axis, [(i, (i + shift) % SIDE) for i in range(SIDE)])]
    unnamed x62 -> x72, local copies, waits for them, and re-layouts: 7.52 us -> 8.18 us
  transfers between devices with their start and end apart: 32 -> 35, of which waited for: 17 -> 13; matrix products, arithmetic and copies ran while one was open for 0% -> 0% of each run, Pallas kernels for 22% -> 23%
where the time goes in v1:
time: 159 us
  waiting for transfers between devices  46.9 us (29%)
  starting transfers between devices  46.6 us (29%)
  Pallas kernels  42.5 us (27%)
  between operations  14.4 us (9%)
  local copies, waits for them, and re-layouts  8.18 us (5%)
    pallas_call x2, Pallas kernels, attend(): pl.pallas_call(attend_kernel, in_specs=[in_hbm()] * (1 + 2 * SIDE) + [any...  21.3 us
    ppermute x7, waiting for transfers between devices, ring(): lax.ppermute(array, 'head', [(i, (i + shift) % HEAD) for i in range(HEAD)])  19.2 us
    ppermute x15, starting transfers between devices, along(): lax.ppermute(array, axis, [(i, (i + shift) % SIDE) for i in range(SIDE)])  18.6 us
    all_to_all x1, waiting for transfers between devices, local(): sums = lax.all_to_all(sums, 'head', 0, 0, tiled=True)  17.1 us
    ppermute x10, starting transfers between devices, swap(): return lax.ppermute(array, 'branch', [(0, 1), (1, 0)])  13.9 us
    ppermute x7, starting transfers between devices, ring(): lax.ppermute(array, 'head', [(i, (i + shift) % HEAD) for i in range(HEAD)])  9.35 us
    unnamed x72, local copies, waits for them, and re-layouts  8.18 us
    pallas_call x1, Pallas kernels, project(): pl.pallas_call(project_kernel, in_specs=[scalars()] * 2 + [in_hbm()] * le...  6.23 us
  transfers between devices with their start and end apart: 35, of which 13 were waited for; matrix products, arithmetic and copies ran while one was open for 0% of the time, Pallas kernels for 23%

profile of v1, /device:TPU:1, one launch (start us, length us, event | category | flops | bytes accessed | tf_op | source)
XLA Modules:
  0.0 158.5 jit_solution(7175178651281398720)
XLA Ops:
  7.2 3.6 %pick.1 = (bf16[256,384]{1,0:T(8,128)(2,1)}, bf16[768,256]{1,0:T(8,128)(2,1)}, bf16[768,256]{1,0:T(8,128)(2,1)}) custom-call(s32[1,2]{1,0:T(1,128)} %blocks_ref.7, s32[1]{0:T(128)S(6)} %copy.16.counts_ref, bf16[1024,384]{1,0:T(8,128)(2,1)} %bitcast.8, bf16[1024,256]{1,0:T(8,128)(2,1)} %bitcast.20, bf16[1024,256]{1,0:T(8,128)(2,1)} %bitcast.22), custom_call_target="tpu_custom_call" | custom-call | tf_op jit(solution)/shard_map/pick/pallas_call | solution.py:91
  10.9 3.3 %collective-permute-start.10 = (bf16[3,1536,256]{2,1,0:T(8,128)(2,1)}, bf16[3,1536,256]{2,1,0:T(8,128)(2,1)}, u32[]{:S(2)}, u32[]{:S(2)}) collective-permute-start(bf16[3,1536,256]{2,1,0:T(8,128)(2,1)} %bitcast.18), channel_id=1, source_target_pairs={{0,128},{128,0},{1,129},{129,1},{2,130},{130,2},{3,131},{131,3},{4... | collective-permute-start | bytes 7077896 | tf_op jit(solution)/shard_map/ppermute | solution.py:486
  14.8 3.9 %collective-permute-start.7 = (bf16[256,384]{1,0:T(8,128)(2,1)}, bf16[256,384]{1,0:T(8,128)(2,1)S(1)}, u32[]{:S(2)}, u32[]{:S(2)}) collective-permute-start(bf16[256,384]{1,0:T(8,128)(2,1)} %get-tuple-element.29.refs_0_), channel_id=1, source_target_pairs={{0,112},{16,0},{32,16},{48,32},{64,48},{80,64},{96,80},{112,96},{1... | collective-permute-start | bytes 589832 | tf_op jit(solution)/shard_map/ppermute | solution.py:482
  18.8 5.3 %collective-permute-done.3.refs_1_ = bf16[256,384]{1,0:T(8,128)(2,1)S(1)} collective-permute-done((bf16[256,384]{1,0:T(8,128)(2,1)}, bf16[256,384]{1,0:T(8,128)(2,1)S(1)}, u32[]{:S(2)}, u32[]{:S(2)}) %collective-permute-start.3) | collective-permute-done | bytes 196640 | tf_op jit(solution)/shard_map/ppermute | solution.py:482
  24.1 2.7 %collective-permute-start.8 = (bf16[256,384]{1,0:T(8,128)(2,1)S(1)}, bf16[256,384]{1,0:T(8,128)(2,1)S(1)}, u32[]{:S(2)}, u32[]{:S(2)}) collective-permute-start(bf16[256,384]{1,0:T(8,128)(2,1)S(1)} %collective-permute-done.7.refs_7_), channel_id=1, source_target_pairs={{0,112},{16,0},{32,16},{48,32},{64,48},{80,64},{96,80},{112,96},{1... | collective-permute-start | bytes 589832 | tf_op jit(solution)/shard_map/ppermute | solution.py:482
  26.7 4.3 %collective-permute-done.4.refs_2_ = bf16[256,384]{1,0:T(8,128)(2,1)S(1)} collective-permute-done((bf16[256,384]{1,0:T(8,128)(2,1)S(1)}, bf16[256,384]{1,0:T(8,128)(2,1)S(1)}, u32[]{:S(2)}, u32[]{:S(2)}) %collective-permute-start.4) | collective-permute-done | bytes 196640 | tf_op jit(solution)/shard_map/ppermute | solution.py:482
  31.0 2.7 %collective-permute-start.9 = (bf16[256,384]{1,0:T(8,128)(2,1)S(1)}, bf16[256,384]{1,0:T(8,128)(2,1)S(1)}, u32[]{:S(2)}, u32[]{:S(2)}) collective-permute-start(bf16[256,384]{1,0:T(8,128)(2,1)S(1)} %collective-permute-done.8.refs_6_), channel_id=1, source_target_pairs={{0,112},{16,0},{32,16},{48,32},{64,48},{80,64},{96,80},{112,96},{1... | collective-permute-start | bytes 589832 | tf_op jit(solution)/shard_map/ppermute | solution.py:482
  33.7 3.5 %collective-permute-done.5.refs_3_ = bf16[256,384]{1,0:T(8,128)(2,1)S(1)} collective-permute-done((bf16[256,384]{1,0:T(8,128)(2,1)S(1)}, bf16[256,384]{1,0:T(8,128)(2,1)S(1)}, u32[]{:S(2)}, u32[]{:S(2)}) %collective-permute-start.5) | collective-permute-done | bytes 196640 | tf_op jit(solution)/shard_map/ppermute | solution.py:482
  37.2 6.1 %collective-permute-done.6.refs_4_ = bf16[256,384]{1,0:T(8,128)(2,1)S(1)} collective-permute-done((bf16[256,384]{1,0:T(8,128)(2,1)S(1)}, bf16[256,384]{1,0:T(8,128)(2,1)S(1)}, u32[]{:S(2)}, u32[]{:S(2)}) %collective-permute-start.6) | collective-permute-done | bytes 196640 | tf_op jit(solution)/shard_map/ppermute | solution.py:482
  44.0 6.2 %project.1 = (bf16[256,384]{1,0:T(8,128)(2,1)}, bf16[256,256]{1,0:T(8,128)(2,1)}, bf16[256,128]{1,0:T(8,128)(2,1)}, bf16[256,3072]{1,0:T(8,128)(2,1)}) custom-call(s32[1,2]{1,0:T(1,128)} %blocks_ref.7, s32[1]{0:T(128)S(6)} %copy.16.counts_ref, bf16[256,384]{1,0:T(8,128)(2,1)} %get-tuple-element.29.refs_0_, bf16[256,384]{1,0:T(8,128)(2,1)} %copy-done.14, ...), custom_call_target="tpu_custom_call" | custom-call | flops 1207959552 | bytes 8388608 | tf_op jit(solution)/shard_map/project/pallas_call | solution.py:170
  50.3 1.4 copy-done.5
  51.7 1.5 hidden_units.1
  53.2 3.2 %collective-permute-start.18 = (bf16[128,768]{1,0:T(8,128)(2,1)S(1)}, bf16[128,768]{1,0:T(8,128)(2,1)S(1)}, u32[]{:S(2)}, u32[]{:S(2)}) collective-permute-start(bf16[128,768]{1,0:T(8,128)(2,1)S(1)} %get-tuple-element.34), channel_id=1, source_target_pairs={{0,128},{128,0},{1,129},{129,1},{2,130},{130,2},{3,131},{131,3},{4... | collective-permute-start | bytes 589832 | tf_op jit(solution)/shard_map/ppermute | solution.py:486
  56.4 1.3 collective-permute-start.14
  57.7 2.6 %collective-permute-start.15 = (bf16[256,128]{1,0:T(8,128)(2,1)S(1)}, bf16[256,128]{1,0:T(8,128)(2,1)S(1)}, u32[]{:S(2)}, u32[]{:S(2)}) collective-permute-start(bf16[256,128]{1,0:T(8,128)(2,1)S(1)} %copy-done.32), channel_id=1, source_target_pairs={{0,8},{4,12},{8,0},{12,4},{1,9},{5,13},{9,1},{13,5},{2,10},{6,14},... | collective-permute-start | bytes 196616 | tf_op jit(solution)/shard_map/ppermute | solution.py:490
  63.3 2.6 %collective-permute-start.12 = (bf16[256,384]{1,0:T(8,128)(2,1)S(1)}, bf16[256,384]{1,0:T(8,128)(2,1)S(1)}, u32[]{:S(2)}, u32[]{:S(2)}) collective-permute-start(bf16[256,384]{1,0:T(8,128)(2,1)S(1)} %copy-done.21), channel_id=1, source_target_pairs={{0,2},{1,3},{2,0},{3,1},{4,6},{5,7},{6,4},{7,5},{8,10},{9,11},{10,... | collective-permute-start | bytes 589832 | tf_op jit(solution)/shard_map/ppermute | solution.py:490
  66.9 1.3 collective-permute-start.30
  69.2 3.1 %units_out.1.refs_9_.base_ref = f32[8,128,384]{2,1,0:T(8,128)S(1)} custom-call(bf16[128,768]{1,0:T(8,128)(2,1)S(1)} %get-tuple-element.33.mine_ref, bf16[128,768]{1,0:T(8,128)(2,1)S(1)} %collective-permute-done.18.theirs_ref, bf16[768,1536]{1,0:T(8,128)(2,1)S(1)} %copy-done.4, bf16[768,1536]{1,0:T(8,128)(2,1)} %collective-permute-done.19.other_ref, ...), custom_call_target="tpu_custom_call" | custom-call | flops 1207959552 | bytes 6291456 | tf_op jit(solution)/shard_map/units_out/pallas_call | solution.py:258
  74.0 2.6 %collective-permute-start.24 = (bf16[256,256]{1,0:T(8,128)(2,1)S(1)}, bf16[256,256]{1,0:T(8,128)(2,1)S(1)}, u32[]{:S(2)}, u32[]{:S(2)}) collective-permute-start(bf16[256,256]{1,0:T(8,128)(2,1)S(1)} %copy-done.25), channel_id=1, source_target_pairs={{0,8},{4,12},{8,0},{12,4},{1,9},{5,13},{9,1},{13,5},{2,10},{6,14},... | collective-permute-start | bytes 393224 | tf_op jit(solution)/shard_map/ppermute | solution.py:490
  78.0 10.6 %attend_first.1 = (bf16[272,128]{1,0:T(8,128)(2,1)}, bf16[272,128]{1,0:T(8,128)(2,1)}, bf16[272,128]{1,0:T(8,128)(2,1)}, bf16[272,128]{1,0:T(8,128)(2,1)}) custom-call(bf16[3072,256]{1,0:T(8,128)(2,1)} %all-gather.3.cloned.1.call-done.refs_0_, bf16[256,384]{1,0:T(8,128)(2,1)} %get-tuple-element.30.refs_1_.refs_5_, bf16[256,384]{1,0:T(8,128)(2,1)} %copy-done.22, ...), custom_call_target="tpu_custom_call" | custom-call | flops 2147483648 | bytes 4194304 | tf_op jit(solution)/shard_map/attend_first/pallas_call | solution.py:338
  89.5 10.7 %attend_second.1 = (bf16[272,128]{1,0:T(8,128)(2,1)}, bf16[272,128]{1,0:T(8,128)(2,1)}, bf16[272,128]{1,0:T(8,128)(2,1)}, bf16[272,128]{1,0:T(8,128)(2,1)}) custom-call(bf16[3072,256]{1,0:T(8,128)(2,1)} %all-gather.5.cloned.1.call-done.refs_0_, bf16[256,256]{1,0:T(8,128)(2,1)} %get-tuple-element.40.refs_1_, bf16[256,256]{1,0:T(8,128)(2,1)} %copy-done.26, ...), custom_call_target="tpu_custom_call" | custom-call | flops 2147483648 | bytes 4194304 | tf_op jit(solution)/shard_map/attend_second/pallas_call | solution.py:338
  100.2 1.5 collective-permute-start.26
  103.6 1.8 %collective-permute-start.21 = (bf16[272,128]{1,0:T(8,128)(2,1)S(1)}, bf16[272,128]{1,0:T(8,128)(2,1)S(1)}, u32[]{:S(2)}, u32[]{:S(2)}) collective-permute-start(bf16[272,128]{1,0:T(8,128)(2,1)S(1)} %copy-done.30), channel_id=1, source_target_pairs={{0,8},{4,12},{8,0},{12,4},{1,9},{5,13},{9,1},{13,5},{2,10},{6,14},... | collective-permute-start | bytes 208904 | tf_op jit(solution)/shard_map/ppermute | solution.py:490
  107.3 1.2 collective-permute-done.21.refs_2_
  108.6 3.0 %collective-permute-done.22.refs_3_ = bf16[272,128]{1,0:T(8,128)(2,1)S(1)} collective-permute-done((bf16[272,128]{1,0:T(8,128)(2,1)S(1)}, bf16[272,128]{1,0:T(8,128)(2,1)S(1)}, u32[]{:S(2)}, u32[]{:S(2)}) %collective-permute-start.22) | collective-permute-done | bytes 69664 | tf_op jit(solution)/shard_map/ppermute | solution.py:490
  113.6 3.4 %collective-permute-start.29 = (bf16[128,256]{1,0:T(8,128)(2,1)S(1)}, bf16[128,256]{1,0:T(8,128)(2,1)S(1)}, u32[]{:S(2)}, u32[]{:S(2)}) collective-permute-start(bf16[128,256]{1,0:T(8,128)(2,1)S(1)} %get-tuple-element.46), channel_id=1, source_target_pairs={{0,128},{128,0},{1,129},{129,1},{2,130},{130,2},{3,131},{131,3},{4... | collective-permute-start | bytes 196616 | tf_op jit(solution)/shard_map/ppermute | solution.py:486
  119.1 1.5 heads_out.1
  120.6 4.6 %all-to-all-start = ((bf16[8,128,384]{2,1,0:T(8,128)(2,1)}), bf16[8,128,384]{2,1,0:T(8,128)(2,1)S(1)}, u32[]{:S(2)}, u32[]{:S(2)}) async-start(bf16[8,128,384]{2,1,0:T(8,128)(2,1)} %heads_out.1), calls=%async_computation | async-start | bytes 1572864 | tf_op jit(solution)/shard_map/all_to_all | solution.py:564
  126.1 1.8 %collective-permute-done.1.other_ref = bf16[1024,384]{1,0:T(8,128)(2,1)S(1)} collective-permute-done((bf16[1024,384]{1,0:T(8,128)(2,1)S(1)}, bf16[1024,384]{1,0:T(8,128)(2,1)S(1)}, u32[]{:S(2)}, u32[]{:S(2)}) %collective-permute-start.1) | collective-permute-done | bytes 786464 | tf_op jit(solution)/shard_map/ppermute | solution.py:486
  129.0 2.7 %stale_rows.1 = (bf16[1024,384]{1,0:T(8,128)(2,1)}, f32[128,384]{1,0:T(8,128)S(1)}, bf16[128,384]{1,0:T(8,128)(2,1)S(1)}) custom-call(s32[1,2]{1,0:T(1,128)S(1)} %copy-done.13, f32[3,1,3072]{2,1,0:T(1,128)S(1)} %bitcast.17, f32[3,1,3072]{2,1,0:T(1,128)S(1)} %collective-permute-done.mod_other_ref, bf16[1024,384]{1,0:T(8,128)(2,1)S(1)} %bitcast.10, ...), custom_call_target="tpu_custom_call" | custom-call | tf_op jit(solution)/shard_map/stale_rows/pallas_call | solution.py:422
  131.7 17.1 %all-to-all-done.parts_ref = bf16[8,128,384]{2,1,0:T(8,128)(2,1)S(1)} async-done(((bf16[8,128,384]{2,1,0:T(8,128)(2,1)}), bf16[8,128,384]{2,1,0:T(8,128)(2,1)S(1)}, u32[]{:S(2)}, u32[]{:S(2)}) %all-to-all-start) | async-done | bytes 786464 | tf_op jit(solution)/shard_map/all_to_all | solution.py:564
  150.4 1.2 place.1
  (123 shorter events, 21.7 us)
Async XLA Ops:
  6.5 70.2 %all-gather.3.cloned.1.call-start = ((), (), s32[]{:S(2)}) async-start(), calls=%async_computation.1 | async-start | bytes 1966080 | tf_op jit(solution)/shard_map/all_gather | solution.py:519
  10.8 77.8 %all-gather.5.cloned.1.call-start = ((), (), s32[]{:S(2)}) async-start(), calls=%async_computation.2 | async-start | bytes 1966080 | tf_op jit(solution)/shard_map/all_gather | solution.py:520
  10.9 32.4 %collective-permute-start.10 = (bf16[3,1536,256]{2,1,0:T(8,128)(2,1)}, bf16[3,1536,256]{2,1,0:T(8,128)(2,1)}, u32[]{:S(2)}, u32[]{:S(2)}) collective-permute-start(bf16[3,1536,256]{2,1,0:T(8,128)(2,1)} %bitcast.18), channel_id=1, source_target_pairs={{0,128},{128,0},{1,129},{129,1},{2,130},{130,2},{3,131},{131,3},{4... | collective-permute-start | bytes 7077896 | tf_op jit(solution)/shard_map/ppermute | solution.py:486
  14.2 36.0 %collective-permute-start.17 = (bf16[1536,768]{1,0:T(8,128)(2,1)}, bf16[1536,768]{1,0:T(8,128)(2,1)S(1)}, u32[]{:S(2)}, u32[]{:S(2)}) collective-permute-start(bf16[1536,768]{1,0:T(8,128)(2,1)} %own_ref.3), channel_id=1, source_target_pairs={{0,128},{128,0},{1,129},{129,1},{2,130},{130,2},{3,131},{131,3},{4... | collective-permute-start | bytes 7077896 | tf_op jit(solution)/shard_map/ppermute | solution.py:486
  14.3 48.9 %collective-permute-start.19 = (bf16[768,1536]{1,0:T(8,128)(2,1)}, bf16[768,1536]{1,0:T(8,128)(2,1)}, u32[]{:S(2)}, u32[]{:S(2)}) collective-permute-start(bf16[768,1536]{1,0:T(8,128)(2,1)} %own_ref.4), channel_id=1, source_target_pairs={{0,128},{128,0},{1,129},{129,1},{2,130},{130,2},{3,131},{131,3},{4... | collective-permute-start | bytes 7077896 | tf_op jit(solution)/shard_map/ppermute | solution.py:486
  14.7 9.3 %collective-permute-start.3 = (bf16[256,384]{1,0:T(8,128)(2,1)}, bf16[256,384]{1,0:T(8,128)(2,1)S(1)}, u32[]{:S(2)}, u32[]{:S(2)}) collective-permute-start(bf16[256,384]{1,0:T(8,128)(2,1)} %get-tuple-element.29.refs_0_), channel_id=1, source_target_pairs={{0,16},{16,32},{32,48},{48,64},{64,80},{80,96},{96,112},{112,0},{1... | collective-permute-start | bytes 589832 | tf_op jit(solution)/shard_map/ppermute | solution.py:482
  14.8 9.2 %collective-permute-start.7 = (bf16[256,384]{1,0:T(8,128)(2,1)}, bf16[256,384]{1,0:T(8,128)(2,1)S(1)}, u32[]{:S(2)}, u32[]{:S(2)}) collective-permute-start(bf16[256,384]{1,0:T(8,128)(2,1)} %get-tuple-element.29.refs_0_), channel_id=1, source_target_pairs={{0,112},{16,0},{32,16},{48,32},{64,48},{80,64},{96,80},{112,96},{1... | collective-permute-start | bytes 589832 | tf_op jit(solution)/shard_map/ppermute | solution.py:482
  24.0 7.0 %collective-permute-start.4 = (bf16[256,384]{1,0:T(8,128)(2,1)S(1)}, bf16[256,384]{1,0:T(8,128)(2,1)S(1)}, u32[]{:S(2)}, u32[]{:S(2)}) collective-permute-start(bf16[256,384]{1,0:T(8,128)(2,1)S(1)} %collective-permute-done.3.refs_1_), channel_id=1, source_target_pairs={{0,16},{16,32},{32,48},{48,64},{64,80},{80,96},{96,112},{112,0},{1... | collective-permute-start | bytes 589832 | tf_op jit(solution)/shard_map/ppermute | solution.py:482
  24.1 7.0 %collective-permute-start.8 = (bf16[256,384]{1,0:T(8,128)(2,1)S(1)}, bf16[256,384]{1,0:T(8,128)(2,1)S(1)}, u32[]{:S(2)}, u32[]{:S(2)}) collective-permute-start(bf16[256,384]{1,0:T(8,128)(2,1)S(1)} %collective-permute-done.7.refs_7_), channel_id=1, source_target_pairs={{0,112},{16,0},{32,16},{48,32},{64,48},{80,64},{96,80},{112,96},{1... | collective-permute-start | bytes 589832 | tf_op jit(solution)/shard_map/ppermute | solution.py:482
  31.0 6.2 %collective-permute-start.5 = (bf16[256,384]{1,0:T(8,128)(2,1)S(1)}, bf16[256,384]{1,0:T(8,128)(2,1)S(1)}, u32[]{:S(2)}, u32[]{:S(2)}) collective-permute-start(bf16[256,384]{1,0:T(8,128)(2,1)S(1)} %collective-permute-done.4.refs_2_), channel_id=1, source_target_pairs={{0,16},{16,32},{32,48},{48,64},{64,80},{80,96},{96,112},{112,0},{1... | collective-permute-start | bytes 589832 | tf_op jit(solution)/shard_map/ppermute | solution.py:482
  31.0 6.1 %collective-permute-start.9 = (bf16[256,384]{1,0:T(8,128)(2,1)S(1)}, bf16[256,384]{1,0:T(8,128)(2,1)S(1)}, u32[]{:S(2)}, u32[]{:S(2)}) collective-permute-start(bf16[256,384]{1,0:T(8,128)(2,1)S(1)} %collective-permute-done.8.refs_6_), channel_id=1, source_target_pairs={{0,112},{16,0},{32,16},{48,32},{64,48},{80,64},{96,80},{112,96},{1... | collective-permute-start | bytes 589832 | tf_op jit(solution)/shard_map/ppermute | solution.py:482
  37.2 6.1 %collective-permute-start.6 = (bf16[256,384]{1,0:T(8,128)(2,1)S(1)}, bf16[256,384]{1,0:T(8,128)(2,1)S(1)}, u32[]{:S(2)}, u32[]{:S(2)}) collective-permute-start(bf16[256,384]{1,0:T(8,128)(2,1)S(1)} %collective-permute-done.5.refs_3_), channel_id=1, source_target_pairs={{0,16},{16,32},{32,48},{48,64},{64,80},{80,96},{96,112},{112,0},{1... | collective-permute-start | bytes 589832 | tf_op jit(solution)/shard_map/ppermute | solution.py:482
  53.2 14.9 %collective-permute-start.18 = (bf16[128,768]{1,0:T(8,128)(2,1)S(1)}, bf16[128,768]{1,0:T(8,128)(2,1)S(1)}, u32[]{:S(2)}, u32[]{:S(2)}) collective-permute-start(bf16[128,768]{1,0:T(8,128)(2,1)S(1)} %get-tuple-element.34), channel_id=1, source_target_pairs={{0,128},{128,0},{1,129},{129,1},{2,130},{130,2},{3,131},{131,3},{4... | collective-permute-start | bytes 589832 | tf_op jit(solution)/shard_map/ppermute | solution.py:486
  56.4 9.4 %collective-permute-start.14 = (bf16[256,128]{1,0:T(8,128)(2,1)S(1)}, bf16[256,128]{1,0:T(8,128)(2,1)S(1)}, u32[]{:S(2)}, u32[]{:S(2)}) collective-permute-start(bf16[256,128]{1,0:T(8,128)(2,1)S(1)} %copy-done.32), channel_id=1, source_target_pairs={{0,4},{4,8},{8,12},{12,0},{1,5},{5,9},{9,13},{13,1},{2,6},{6,10},{... | collective-permute-start | bytes 196616 | tf_op jit(solution)/shard_map/ppermute | solution.py:490
  57.7 9.2 %collective-permute-start.15 = (bf16[256,128]{1,0:T(8,128)(2,1)S(1)}, bf16[256,128]{1,0:T(8,128)(2,1)S(1)}, u32[]{:S(2)}, u32[]{:S(2)}) collective-permute-start(bf16[256,128]{1,0:T(8,128)(2,1)S(1)} %copy-done.32), channel_id=1, source_target_pairs={{0,8},{4,12},{8,0},{12,4},{1,9},{5,13},{9,1},{13,5},{2,10},{6,14},... | collective-permute-start | bytes 196616 | tf_op jit(solution)/shard_map/ppermute | solution.py:490
  62.0 12.0 %collective-permute-start.11 = (bf16[256,384]{1,0:T(8,128)(2,1)S(1)}, bf16[256,384]{1,0:T(8,128)(2,1)S(1)}, u32[]{:S(2)}, u32[]{:S(2)}) collective-permute-start(bf16[256,384]{1,0:T(8,128)(2,1)S(1)} %copy-done.21), channel_id=1, source_target_pairs={{0,1},{1,2},{2,3},{3,0},{4,5},{5,6},{6,7},{7,4},{8,9},{9,10},{10,1... | collective-permute-start | bytes 589832 | tf_op jit(solution)/shard_map/ppermute | solution.py:490
  63.3 13.4 %collective-permute-start.12 = (bf16[256,384]{1,0:T(8,128)(2,1)S(1)}, bf16[256,384]{1,0:T(8,128)(2,1)S(1)}, u32[]{:S(2)}, u32[]{:S(2)}) collective-permute-start(bf16[256,384]{1,0:T(8,128)(2,1)S(1)} %copy-done.21), channel_id=1, source_target_pairs={{0,2},{1,3},{2,0},{3,1},{4,6},{5,7},{6,4},{7,5},{8,10},{9,11},{10,... | collective-permute-start | bytes 589832 | tf_op jit(solution)/shard_map/ppermute | solution.py:490
  65.8 10.9 %collective-permute-start.13 = (bf16[256,384]{1,0:T(8,128)(2,1)S(1)}, bf16[256,384]{1,0:T(8,128)(2,1)S(1)}, u32[]{:S(2)}, u32[]{:S(2)}) collective-permute-start(bf16[256,384]{1,0:T(8,128)(2,1)S(1)} %copy-done.21), channel_id=1, source_target_pairs={{0,3},{1,0},{2,1},{3,2},{4,7},{5,4},{6,5},{7,6},{8,11},{9,8},{10,9... | collective-permute-start | bytes 589832 | tf_op jit(solution)/shard_map/ppermute | solution.py:490
  66.9 50.2 %collective-permute-start.30 = (bf16[256,1536]{1,0:T(8,128)(2,1)S(1)}, bf16[256,1536]{1,0:T(8,128)(2,1)S(1)}, u32[]{:S(2)}, u32[]{:S(2)}) collective-permute-start(bf16[256,1536]{1,0:T(8,128)(2,1)S(1)} %copy-done.7), channel_id=1, source_target_pairs={{0,128},{128,0},{1,129},{129,1},{2,130},{130,2},{3,131},{131,3},{4... | collective-permute-start | bytes 2359304 | tf_op jit(solution)/shard_map/ppermute | solution.py:486
  68.2 5.4 %collective-permute-start.16 = (bf16[256,128]{1,0:T(8,128)(2,1)S(1)}, bf16[256,128]{1,0:T(8,128)(2,1)S(1)}, u32[]{:S(2)}, u32[]{:S(2)}) collective-permute-start(bf16[256,128]{1,0:T(8,128)(2,1)S(1)} %copy-done.32), channel_id=1, source_target_pairs={{0,12},{4,0},{8,4},{12,8},{1,13},{5,1},{9,5},{13,9},{2,14},{6,2},{... | collective-permute-start | bytes 196616 | tf_op jit(solution)/shard_map/ppermute | solution.py:490
  73.5 15.1 %collective-permute-start.23 = (bf16[256,256]{1,0:T(8,128)(2,1)S(1)}, bf16[256,256]{1,0:T(8,128)(2,1)S(1)}, u32[]{:S(2)}, u32[]{:S(2)}) collective-permute-start(bf16[256,256]{1,0:T(8,128)(2,1)S(1)} %copy-done.25), channel_id=1, source_target_pairs={{0,4},{4,8},{8,12},{12,0},{1,5},{5,9},{9,13},{13,1},{2,6},{6,10},{... | collective-permute-start | bytes 393224 | tf_op jit(solution)/shard_map/ppermute | solution.py:490
  74.0 14.7 %collective-permute-start.24 = (bf16[256,256]{1,0:T(8,128)(2,1)S(1)}, bf16[256,256]{1,0:T(8,128)(2,1)S(1)}, u32[]{:S(2)}, u32[]{:S(2)}) collective-permute-start(bf16[256,256]{1,0:T(8,128)(2,1)S(1)} %copy-done.25), channel_id=1, source_target_pairs={{0,8},{4,12},{8,0},{12,4},{1,9},{5,13},{9,1},{13,5},{2,10},{6,14},... | collective-permute-start | bytes 393224 | tf_op jit(solution)/shard_map/ppermute | solution.py:490
  76.7 12.0 %collective-permute-start.25 = (bf16[256,256]{1,0:T(8,128)(2,1)S(1)}, bf16[256,256]{1,0:T(8,128)(2,1)S(1)}, u32[]{:S(2)}, u32[]{:S(2)}) collective-permute-start(bf16[256,256]{1,0:T(8,128)(2,1)S(1)} %copy-done.25), channel_id=1, source_target_pairs={{0,12},{4,0},{8,4},{12,8},{1,13},{5,1},{9,5},{13,9},{2,14},{6,2},{... | collective-permute-start | bytes 393224 | tf_op jit(solution)/shard_map/ppermute | solution.py:490
  100.2 3.4 %collective-permute-start.26 = (bf16[272,128]{1,0:T(8,128)(2,1)}, bf16[272,128]{1,0:T(8,128)(2,1)S(1)}, u32[]{:S(2)}, u32[]{:S(2)}) collective-permute-start(bf16[272,128]{1,0:T(8,128)(2,1)} %get-tuple-element.42), channel_id=1, source_target_pairs={{0,3},{1,0},{2,1},{3,2},{4,7},{5,4},{6,5},{7,6},{8,11},{9,8},{10,9... | collective-permute-start | bytes 208904 | tf_op jit(solution)/shard_map/ppermute | solution.py:490
  101.6 4.9 %collective-permute-start.27 = (bf16[272,128]{1,0:T(8,128)(2,1)}, bf16[272,128]{1,0:T(8,128)(2,1)S(1)}, u32[]{:S(2)}, u32[]{:S(2)}) collective-permute-start(bf16[272,128]{1,0:T(8,128)(2,1)} %get-tuple-element.43), channel_id=1, source_target_pairs={{0,2},{1,3},{2,0},{3,1},{4,6},{5,7},{6,4},{7,5},{8,10},{9,11},{10,... | collective-permute-start | bytes 208904 | tf_op jit(solution)/shard_map/ppermute | solution.py:490
  102.6 4.7 %collective-permute-start.28 = (bf16[272,128]{1,0:T(8,128)(2,1)}, bf16[272,128]{1,0:T(8,128)(2,1)S(1)}, u32[]{:S(2)}, u32[]{:S(2)}) collective-permute-start(bf16[272,128]{1,0:T(8,128)(2,1)} %get-tuple-element.44), channel_id=1, source_target_pairs={{0,1},{1,2},{2,3},{3,0},{4,5},{5,6},{6,7},{7,4},{8,9},{9,10},{10,1... | collective-permute-start | bytes 208904 | tf_op jit(solution)/shard_map/ppermute | solution.py:490
  102.8 4.6 %collective-permute-start.20 = (bf16[272,128]{1,0:T(8,128)(2,1)S(1)}, bf16[272,128]{1,0:T(8,128)(2,1)S(1)}, u32[]{:S(2)}, u32[]{:S(2)}) collective-permute-start(bf16[272,128]{1,0:T(8,128)(2,1)S(1)} %copy-done.31), channel_id=1, source_target_pairs={{0,12},{4,0},{8,4},{12,8},{1,13},{5,1},{9,5},{13,9},{2,14},{6,2},{... | collective-permute-start | bytes 208904 | tf_op jit(solution)/shard_map/ppermute | solution.py:490
  103.6 5.0 %collective-permute-start.21 = (bf16[272,128]{1,0:T(8,128)(2,1)S(1)}, bf16[272,128]{1,0:T(8,128)(2,1)S(1)}, u32[]{:S(2)}, u32[]{:S(2)}) collective-permute-start(bf16[272,128]{1,0:T(8,128)(2,1)S(1)} %copy-done.30), channel_id=1, source_target_pairs={{0,8},{4,12},{8,0},{12,4},{1,9},{5,13},{9,1},{13,5},{2,10},{6,14},... | collective-permute-start | bytes 208904 | tf_op jit(solution)/shard_map/ppermute | solution.py:490
  106.5 5.1 %collective-permute-start.22 = (bf16[272,128]{1,0:T(8,128)(2,1)S(1)}, bf16[272,128]{1,0:T(8,128)(2,1)S(1)}, u32[]{:S(2)}, u32[]{:S(2)}) collective-permute-start(bf16[272,128]{1,0:T(8,128)(2,1)S(1)} %copy-done.29), channel_id=1, source_target_pairs={{0,4},{4,8},{8,12},{12,0},{1,5},{5,9},{9,13},{13,1},{2,6},{6,10},{... | collective-permute-start | bytes 208904 | tf_op jit(solution)/shard_map/ppermute | solution.py:490
  113.6 4.3 %collective-permute-start.29 = (bf16[128,256]{1,0:T(8,128)(2,1)S(1)}, bf16[128,256]{1,0:T(8,128)(2,1)S(1)}, u32[]{:S(2)}, u32[]{:S(2)}) collective-permute-start(bf16[128,256]{1,0:T(8,128)(2,1)S(1)} %get-tuple-element.46), channel_id=1, source_target_pairs={{0,128},{128,0},{1,129},{129,1},{2,130},{130,2},{3,131},{131,3},{4... | collective-permute-start | bytes 196616 | tf_op jit(solution)/shard_map/ppermute | solution.py:486
  120.6 28.2 %all-to-all-start = ((bf16[8,128,384]{2,1,0:T(8,128)(2,1)}), bf16[8,128,384]{2,1,0:T(8,128)(2,1)S(1)}, u32[]{:S(2)}, u32[]{:S(2)}) async-start(bf16[8,128,384]{2,1,0:T(8,128)(2,1)} %heads_out.1), calls=%async_computation | async-start | bytes 1572864 | tf_op jit(solution)/shard_map/all_to_all | solution.py:564
  125.9 3.0 %collective-permute-start.2 = (bf16[1024,384]{1,0:T(8,128)(2,1)S(1)}, bf16[1024,384]{1,0:T(8,128)(2,1)S(1)}, u32[]{:S(2)}, u32[]{:S(2)}) collective-permute-start(bf16[1024,384]{1,0:T(8,128)(2,1)S(1)} %bitcast.11), channel_id=1, source_target_pairs={{0,128},{128,0},{1,129},{129,1},{2,130},{130,2},{3,131},{131,3},{4... | collective-permute-start | bytes 2359304 | tf_op jit(solution)/shard_map/ppermute | solution.py:486
  (39 other events, 294.2 us)
Sparse Core Ops, SparseCore 0:
  10.9 32.8 all-gather.2
  45.6 30.7 all-gather.4
